TPU v7x, 32 devices: a whole 2x2x4 slice. The times are simulated.
32 devices in a mesh: section: 4 (over z), mp: 8 (over y, x, core).
Axes of the slice: x: 2, y: 2, z: 4, core: 2. Of those that a mesh axis runs over, the one named last changes fastest.
Arguments:
- entering_hidden: bfloat16 [4, 256, 8192], P('section', None, 'mp'), may hold values from -12 to 12
- section_weight: bfloat16 [4, 8192, 8192], P('section', None, 'mp'), may hold values from -0.0625 to 0.0625
- section_norm_gain: bfloat16 [4, 8192], P('section', 'mp'), may hold values from 0.5 to 1.5
- plugin_narrowing_factors: bfloat16 [4, 8, 8192, 64], P('section', 'mp'), may hold values from -0.0625 to 0.0625
- plugin_widening_factors: bfloat16 [4, 8, 64, 8192], P('section', 'mp'), may hold values from -0.75 to 0.75
- reward_head: bfloat16 [8192], P('mp'), may hold values from -0.0625 to 0.0625
- adapter_of_block: int32 [4, 2], replicated, may hold values from 0 to 7
- live_block_rows: int32 [4, 2], P('section'), may hold values from 1 to 128
Outputs:
- hidden_out: bfloat16 [4, 256, 8192], P('section', None, 'mp')
- scores: float32 [4, 256], P('section')
All inputs are finite; a program needn't handle non-finite values.
Results may differ from a plain program's by a relative error of at most 0.022.
Values may be sent and summed in bfloat16 or wider, within the bound.
No kernel may reach another device: no remote copies, remote signals or barrier semaphores. Data moves between devices by JAX's collectives and lax.ppermute only.
A program may use at most 64 MiB of HBM per device.

v0:
```python
import jax
import jax.numpy as jnp
from jax import lax
from jax.sharding import PartitionSpec as P

BLOCK = 128


def shifted(value, axis, steps):
    count = lax.axis_size(axis)
    initial, last = (max(0, -steps), min(count, count - steps))
    return lax.ppermute(value, axis, [(source, source + steps) for source in range(initial, last)])


def shards(
    entering_hidden,
    section_weight,
    section_norm_gain,
    plugin_narrowing_factors,
    plugin_widening_factors,
    reward_head,
    adapter_of_block,
    live_block_rows,
):
    sections = lax.axis_size("section")
    section_index = lax.axis_index("section")
    owners = lax.axis_size("mp")
    batches_here, rows, piece_extent = entering_hidden.shape
    micro = batches_here * sections
    width = piece_extent * owners
    blocks = rows // BLOCK
    owned_blocks = plugin_narrowing_factors.shape[1]
    adapters = owned_blocks * owners
    rank_position = plugin_narrowing_factors.shape[3]
    weight = section_weight[0]
    gain = section_norm_gain[0].astype(jnp.float32)
    fed = lax.all_gather(entering_hidden, "section", axis=0, tiled=True)
    up_map_columns = lax.all_to_all(
        plugin_widening_factors, "mp", split_axis=3, concat_axis=1, tiled=True
    )[0]
    up_table = up_map_columns.reshape(adapters, rank_position * piece_extent)
    down_rows = lax.all_to_all(
        plugin_narrowing_factors, "mp", split_axis=2, concat_axis=1, tiled=True
    )[0]
    down_table = down_rows.reshape(adapters, piece_extent * rank_position)

    def layer_of_section(hidden_state, adapter_numbers):
        hidden_f = hidden_state.astype(jnp.float32)
        onehot = (
            adapter_numbers[:, None] == jnp.arange(adapters, dtype=jnp.int32)[None, :]
        ).astype(jnp.bfloat16)
        squares = lax.psum(jnp.sum(hidden_f * hidden_f, axis=1), "mp")
        rescaled_activation = (
            hidden_f * lax.rsqrt(squares / width + 1e-05)[:, None] * gain[None, :]
        ).astype(jnp.bfloat16)
        base = jnp.dot(
            lax.all_gather(rescaled_activation, "mp", axis=1, tiled=True),
            weight,
            preferred_element_type=jnp.float32,
        )
        chosen_down = (
            jnp.dot(onehot, down_table, preferred_element_type=jnp.float32)
            .astype(jnp.bfloat16)
            .reshape(blocks, piece_extent, rank_position)
        )
        compressed_projection = jnp.einsum(
            "brd,bdk->brk",
            rescaled_activation.reshape(blocks, BLOCK, piece_extent),
            chosen_down,
            preferred_element_type=jnp.float32,
        )
        compressed_projection = lax.psum(compressed_projection.astype(jnp.bfloat16), "mp")
        chosen_expansion_matrix = (
            jnp.dot(onehot, up_table, preferred_element_type=jnp.float32)
            .astype(jnp.bfloat16)
            .reshape(blocks, rank_position, piece_extent)
        )
        thin_correction = jnp.einsum(
            "sin,sny->siy",
            compressed_projection,
            chosen_expansion_matrix,
            preferred_element_type=jnp.float32,
        ).reshape(rows, piece_extent)
        return (hidden_f + base + 2.0 * thin_correction).astype(jnp.bfloat16)

    def tick(step, carry):
        moving, finished = carry
        arrived = shifted(moving, "section", 1)
        feed_now = lax.dynamic_index_in_dim(fed, jnp.minimum(step, micro - 1), 0, keepdims=False)
        current_signal = jnp.where(section_index == 0, feed_now, arrived)
        selected_adapter = step - section_index
        valid = (selected_adapter >= 0) & (selected_adapter < micro)
        position = jnp.clip(selected_adapter, 0, micro - 1)
        adapter_numbers = lax.dynamic_index_in_dim(adapter_of_block, position, 0, keepdims=False)
        output = layer_of_section(current_signal, adapter_numbers)
        entry_tuple = valid & (section_index == sections - 1)
        previous = lax.dynamic_index_in_dim(finished, position, 0, keepdims=False)
        finished = lax.dynamic_update_index_in_dim(
            finished, jnp.where(entry_tuple, output, previous), position, 0
        )
        return (output, finished)

    start_moving = jnp.zeros((rows, piece_extent), jnp.bfloat16)
    start_finished = jnp.zeros((micro, rows, piece_extent), jnp.bfloat16)
    moving, finished = lax.fori_loop(0, micro + sections - 1, tick, (start_moving, start_finished))
    hidden_out = lax.psum_scatter(
        finished.astype(jnp.float32).astype(jnp.bfloat16),
        "section",
        scatter_dimension=0,
        tiled=True,
    )
    partial_score = jnp.sum(
        hidden_out.astype(jnp.float32) * reward_head.astype(jnp.float32)[None, None, :], axis=2
    )
    raw = lax.psum(partial_score, "mp")
    place = jnp.arange(rows, dtype=jnp.int32) % BLOCK
    limits = jnp.repeat(live_block_rows, BLOCK, axis=1)
    scores = jnp.where(place[None, :] < limits, raw, jnp.float32(0.0))
    return (hidden_out, scores)


def solution(mesh):
    placed = (
        P("section", None, "mp"),
        P("section", None, "mp"),
        P("section", "mp"),
        P("section", "mp", None, None),
        P("section", "mp", None, None),
        P("mp"),
        P(),
        P("section", None),
    )
    return jax.shard_map(
        shards,
        mesh=mesh,
        in_specs=placed,
        out_specs=(P("section", None, "mp"), P("section", None)),
        check_vma=False,
    )
```

profile of v0, /device:TPU:16, one launch (start us, length us, event | category | flops | bytes accessed | tf_op | source)
XLA Modules:
  0.0 814.6 jit_solution(14217450314727019000)
XLA Ops:
  17.6 45.2 %reduce.3 = bf16[8192,64]{1,0:T(8,128)(2,1)S(1)} reduce(bf16[8192,1,1,64]{3,2,1,0:T(2,128)(2,1)} %bitcast.75, bf16[]{:T(256)} %broadcast.80), dimensions={1,2}, to_apply=%bitcast.30.reduce_sub_computation | reduce | bytes 2097154
  76.2 45.2 %reduce.4 = bf16[8192,64]{1,0:T(8,128)(2,1)S(1)} reduce(bf16[8192,1,1,64]{3,2,1,0:T(2,128)(2,1)} %bitcast.76, bf16[]{:T(256)} %broadcast.80), dimensions={1,2}, to_apply=%bitcast.32.reduce_sub_computation | reduce | bytes 2097154
  132.7 33.1 %bitcast_reduce_fusion = bf16[8192,64]{1,0:T(8,128)(2,1)} fusion(bf16[8192,1,1,64]{3,2,1,0:T(2,128)(2,1)} %reshape.96), kind=kLoop, calls=%fused_computation.28 | loop fusion | bytes 2097152 | tf_op jit(solution)/shard_map/all_to_all | solution.py:42
  184.8 560.8 %while.17 = (s32[]{:T(128)}, bf16[256,1024]{1,0:T(8,128)(2,1)S(1)}, bf16[4,256,1024]{2,1,0:T(8,128)(2,1)}, pred[]{:T(512)}, bf16[4,256,1024]{2,1,0:T(8,128)(2,1)...) while((s32[]{:T(128)}, bf16[256,1024]{1,0:T(8,128)(2,1)S(1)}, ...), condition=%wide.region_4.5_spmd.clone, body=%wide.region_0.4_spmd.clone.sunk | while | flops 4370498048 | bytes 52570532 | solution.py:105
  188.3 12.7 %collective-permute-done = bf16[256,1024]{1,0:T(8,128)(2,1)S(1)} collective-permute-done((bf16[256,1024]{1,0:T(8,128)(2,1)S(1)}, bf16[256,1024]{1,0:T(8,128)(2,1)S(1)}, u32[]{:S(2)}, u32[]{:S(2)}) %collective-permute-start) | collective-permute-done | bytes 524320 | tf_op jit(solution)/shard_map/while/body/eval_jaxpr/ppermute | solution.py:12
  202.3 13.3 %psum.36 = f32[256]{0:T(256)S(1)} all-reduce(f32[256]{0:T(256)S(1)} %get-tuple-element.413), channel_id=1, replica_groups=mesh['section'=4,'mp'=8] {'mp'}, use_global_device_ids=true, to_apply=%region_2.2 | all-reduce | flops 256 | bytes 2048 | tf_op jit(solution)/shard_map/while/body/eval_jaxpr/psum | solution.py:52
  221.4 22.8 %psum.37 = bf16[2,128,64]{1,2,0:T(8,128)(2,1)S(1)} all-reduce(bf16[2,128,64]{1,2,0:T(8,128)(2,1)S(1)} %convolution_convert_fusion.7), channel_id=1, replica_groups=mesh['section'=4,'mp'=8] {'mp'}, use_global_device_ids=true, to_apply=%region_3.3 | all-reduce | flops 16384 | bytes 65536 | tf_op jit(solution)/shard_map/while/body/eval_jaxpr/psum | solution.py:72
  252.9 12.4 %bitcast_dynamic-update-slice_fusion.2 = (bf16[4,256,1024]{2,1,0:T(8,128)(2,1)}, bf16[256,1024]{1,0:T(8,128)(2,1)S(1)}) fusion(bf16[4,256,1024]{2,1,0:T(8,128)(2,1)} %get-tuple-element.434, s32[]{:T(128)S(6)} %min.21, bf16[1,256,1024]{2,1,0:T(8,128)(2,1)} %constant_dynamic-slice_fusion.3, pred[]{:T(512)S(6)} %and.44, f32[256,1024]{1,0:T(8,128)S(1)} %bitcast.73, ...), kind=kOutput, calls=%fused_computation.12.clone.1 | convolution fusion | flops 4296278016 | bytes 24117252 | tf_op jit(solution)/shard_map/while/body/eval_jaxpr/dot_general | solution.py:56
  268.7 12.6 %collective-permute-done = bf16[256,1024]{1,0:T(8,128)(2,1)S(1)} collective-permute-done((bf16[256,1024]{1,0:T(8,128)(2,1)S(1)}, bf16[256,1024]{1,0:T(8,128)(2,1)S(1)}, u32[]{:S(2)}, u32[]{:S(2)}) %collective-permute-start) | collective-permute-done | bytes 524320 | tf_op jit(solution)/shard_map/while/body/eval_jaxpr/ppermute | solution.py:12
  300.7 22.8 %psum.37 = bf16[2,128,64]{1,2,0:T(8,128)(2,1)S(1)} all-reduce(bf16[2,128,64]{1,2,0:T(8,128)(2,1)S(1)} %convolution_convert_fusion.7), channel_id=1, replica_groups=mesh['section'=4,'mp'=8] {'mp'}, use_global_device_ids=true, to_apply=%region_3.3 | all-reduce | flops 16384 | bytes 65536 | tf_op jit(solution)/shard_map/while/body/eval_jaxpr/psum | solution.py:72
  332.9 12.4 %bitcast_dynamic-update-slice_fusion.2 = (bf16[4,256,1024]{2,1,0:T(8,128)(2,1)}, bf16[256,1024]{1,0:T(8,128)(2,1)S(1)}) fusion(bf16[4,256,1024]{2,1,0:T(8,128)(2,1)} %get-tuple-element.434, s32[]{:T(128)S(6)} %min.21, bf16[1,256,1024]{2,1,0:T(8,128)(2,1)} %constant_dynamic-slice_fusion.3, pred[]{:T(512)S(6)} %and.44, f32[256,1024]{1,0:T(8,128)S(1)} %bitcast.73, ...), kind=kOutput, calls=%fused_computation.12.clone.1 | convolution fusion | flops 4296278016 | bytes 24117252 | tf_op jit(solution)/shard_map/while/body/eval_jaxpr/dot_general | solution.py:56
  348.7 12.6 %collective-permute-done = bf16[256,1024]{1,0:T(8,128)(2,1)S(1)} collective-permute-done((bf16[256,1024]{1,0:T(8,128)(2,1)S(1)}, bf16[256,1024]{1,0:T(8,128)(2,1)S(1)}, u32[]{:S(2)}, u32[]{:S(2)}) %collective-permute-start) | collective-permute-done | bytes 524320 | tf_op jit(solution)/shard_map/while/body/eval_jaxpr/ppermute | solution.py:12
  362.6 12.3 %psum.36 = f32[256]{0:T(256)S(1)} all-reduce(f32[256]{0:T(256)S(1)} %get-tuple-element.413), channel_id=1, replica_groups=mesh['section'=4,'mp'=8] {'mp'}, use_global_device_ids=true, to_apply=%region_2.2 | all-reduce | flops 256 | bytes 2048 | tf_op jit(solution)/shard_map/while/body/eval_jaxpr/psum | solution.py:52
  380.8 22.8 %psum.37 = bf16[2,128,64]{1,2,0:T(8,128)(2,1)S(1)} all-reduce(bf16[2,128,64]{1,2,0:T(8,128)(2,1)S(1)} %convolution_convert_fusion.7), channel_id=1, replica_groups=mesh['section'=4,'mp'=8] {'mp'}, use_global_device_ids=true, to_apply=%region_3.3 | all-reduce | flops 16384 | bytes 65536 | tf_op jit(solution)/shard_map/while/body/eval_jaxpr/psum | solution.py:72
  412.9 12.4 %bitcast_dynamic-update-slice_fusion.2 = (bf16[4,256,1024]{2,1,0:T(8,128)(2,1)}, bf16[256,1024]{1,0:T(8,128)(2,1)S(1)}) fusion(bf16[4,256,1024]{2,1,0:T(8,128)(2,1)} %get-tuple-element.434, s32[]{:T(128)S(6)} %min.21, bf16[1,256,1024]{2,1,0:T(8,128)(2,1)} %constant_dynamic-slice_fusion.3, pred[]{:T(512)S(6)} %and.44, f32[256,1024]{1,0:T(8,128)S(1)} %bitcast.73, ...), kind=kOutput, calls=%fused_computation.12.clone.1 | convolution fusion | flops 4296278016 | bytes 24117252 | tf_op jit(solution)/shard_map/while/body/eval_jaxpr/dot_general | solution.py:56
  428.8 12.6 %collective-permute-done = bf16[256,1024]{1,0:T(8,128)(2,1)S(1)} collective-permute-done((bf16[256,1024]{1,0:T(8,128)(2,1)S(1)}, bf16[256,1024]{1,0:T(8,128)(2,1)S(1)}, u32[]{:S(2)}, u32[]{:S(2)}) %collective-permute-start) | collective-permute-done | bytes 524320 | tf_op jit(solution)/shard_map/while/body/eval_jaxpr/ppermute | solution.py:12
  442.7 12.3 %psum.36 = f32[256]{0:T(256)S(1)} all-reduce(f32[256]{0:T(256)S(1)} %get-tuple-element.413), channel_id=1, replica_groups=mesh['section'=4,'mp'=8] {'mp'}, use_global_device_ids=true, to_apply=%region_2.2 | all-reduce | flops 256 | bytes 2048 | tf_op jit(solution)/shard_map/while/body/eval_jaxpr/psum | solution.py:52
  460.8 22.8 %psum.37 = bf16[2,128,64]{1,2,0:T(8,128)(2,1)S(1)} all-reduce(bf16[2,128,64]{1,2,0:T(8,128)(2,1)S(1)} %convolution_convert_fusion.7), channel_id=1, replica_groups=mesh['section'=4,'mp'=8] {'mp'}, use_global_device_ids=true, to_apply=%region_3.3 | all-reduce | flops 16384 | bytes 65536 | tf_op jit(solution)/shard_map/while/body/eval_jaxpr/psum | solution.py:72
  493.0 12.4 %bitcast_dynamic-update-slice_fusion.2 = (bf16[4,256,1024]{2,1,0:T(8,128)(2,1)}, bf16[256,1024]{1,0:T(8,128)(2,1)S(1)}) fusion(bf16[4,256,1024]{2,1,0:T(8,128)(2,1)} %get-tuple-element.434, s32[]{:T(128)S(6)} %min.21, bf16[1,256,1024]{2,1,0:T(8,128)(2,1)} %constant_dynamic-slice_fusion.3, pred[]{:T(512)S(6)} %and.44, f32[256,1024]{1,0:T(8,128)S(1)} %bitcast.73, ...), kind=kOutput, calls=%fused_computation.12.clone.1 | convolution fusion | flops 4296278016 | bytes 24117252 | tf_op jit(solution)/shard_map/while/body/eval_jaxpr/dot_general | solution.py:56
  508.9 12.6 %collective-permute-done = bf16[256,1024]{1,0:T(8,128)(2,1)S(1)} collective-permute-done((bf16[256,1024]{1,0:T(8,128)(2,1)S(1)}, bf16[256,1024]{1,0:T(8,128)(2,1)S(1)}, u32[]{:S(2)}, u32[]{:S(2)}) %collective-permute-start) | collective-permute-done | bytes 524320 | tf_op jit(solution)/shard_map/while/body/eval_jaxpr/ppermute | solution.py:12
  540.9 22.8 %psum.37 = bf16[2,128,64]{1,2,0:T(8,128)(2,1)S(1)} all-reduce(bf16[2,128,64]{1,2,0:T(8,128)(2,1)S(1)} %convolution_convert_fusion.7), channel_id=1, replica_groups=mesh['section'=4,'mp'=8] {'mp'}, use_global_device_ids=true, to_apply=%region_3.3 | all-reduce | flops 16384 | bytes 65536 | tf_op jit(solution)/shard_map/while/body/eval_jaxpr/psum | solution.py:72
  573.1 12.4 %bitcast_dynamic-update-slice_fusion.2 = (bf16[4,256,1024]{2,1,0:T(8,128)(2,1)}, bf16[256,1024]{1,0:T(8,128)(2,1)S(1)}) fusion(bf16[4,256,1024]{2,1,0:T(8,128)(2,1)} %get-tuple-element.434, s32[]{:T(128)S(6)} %min.21, bf16[1,256,1024]{2,1,0:T(8,128)(2,1)} %constant_dynamic-slice_fusion.3, pred[]{:T(512)S(6)} %and.44, f32[256,1024]{1,0:T(8,128)S(1)} %bitcast.73, ...), kind=kOutput, calls=%fused_computation.12.clone.1 | convolution fusion | flops 4296278016 | bytes 24117252 | tf_op jit(solution)/shard_map/while/body/eval_jaxpr/dot_general | solution.py:56
  589.0 12.5 %collective-permute-done = bf16[256,1024]{1,0:T(8,128)(2,1)S(1)} collective-permute-done((bf16[256,1024]{1,0:T(8,128)(2,1)S(1)}, bf16[256,1024]{1,0:T(8,128)(2,1)S(1)}, u32[]{:S(2)}, u32[]{:S(2)}) %collective-permute-start) | collective-permute-done | bytes 524320 | tf_op jit(solution)/shard_map/while/body/eval_jaxpr/ppermute | solution.py:12
  602.8 12.3 %psum.36 = f32[256]{0:T(256)S(1)} all-reduce(f32[256]{0:T(256)S(1)} %get-tuple-element.413), channel_id=1, replica_groups=mesh['section'=4,'mp'=8] {'mp'}, use_global_device_ids=true, to_apply=%region_2.2 | all-reduce | flops 256 | bytes 2048 | tf_op jit(solution)/shard_map/while/body/eval_jaxpr/psum | solution.py:52
  620.9 22.8 %psum.37 = bf16[2,128,64]{1,2,0:T(8,128)(2,1)S(1)} all-reduce(bf16[2,128,64]{1,2,0:T(8,128)(2,1)S(1)} %convolution_convert_fusion.7), channel_id=1, replica_groups=mesh['section'=4,'mp'=8] {'mp'}, use_global_device_ids=true, to_apply=%region_3.3 | all-reduce | flops 16384 | bytes 65536 | tf_op jit(solution)/shard_map/while/body/eval_jaxpr/psum | solution.py:72
  653.2 12.4 %bitcast_dynamic-update-slice_fusion.2 = (bf16[4,256,1024]{2,1,0:T(8,128)(2,1)}, bf16[256,1024]{1,0:T(8,128)(2,1)S(1)}) fusion(bf16[4,256,1024]{2,1,0:T(8,128)(2,1)} %get-tuple-element.434, s32[]{:T(128)S(6)} %min.21, bf16[1,256,1024]{2,1,0:T(8,128)(2,1)} %constant_dynamic-slice_fusion.3, pred[]{:T(512)S(6)} %and.44, f32[256,1024]{1,0:T(8,128)S(1)} %bitcast.73, ...), kind=kOutput, calls=%fused_computation.12.clone.1 | convolution fusion | flops 4296278016 | bytes 24117252 | tf_op jit(solution)/shard_map/while/body/eval_jaxpr/dot_general | solution.py:56
  669.0 12.6 %collective-permute-done = bf16[256,1024]{1,0:T(8,128)(2,1)S(1)} collective-permute-done((bf16[256,1024]{1,0:T(8,128)(2,1)S(1)}, bf16[256,1024]{1,0:T(8,128)(2,1)S(1)}, u32[]{:S(2)}, u32[]{:S(2)}) %collective-permute-start) | collective-permute-done | bytes 524320 | tf_op jit(solution)/shard_map/while/body/eval_jaxpr/ppermute | solution.py:12
  682.9 12.3 %psum.36 = f32[256]{0:T(256)S(1)} all-reduce(f32[256]{0:T(256)S(1)} %get-tuple-element.413), channel_id=1, replica_groups=mesh['section'=4,'mp'=8] {'mp'}, use_global_device_ids=true, to_apply=%region_2.2 | all-reduce | flops 256 | bytes 2048 | tf_op jit(solution)/shard_map/while/body/eval_jaxpr/psum | solution.py:52
  701.0 22.8 %psum.37 = bf16[2,128,64]{1,2,0:T(8,128)(2,1)S(1)} all-reduce(bf16[2,128,64]{1,2,0:T(8,128)(2,1)S(1)} %convolution_convert_fusion.7), channel_id=1, replica_groups=mesh['section'=4,'mp'=8] {'mp'}, use_global_device_ids=true, to_apply=%region_3.3 | all-reduce | flops 16384 | bytes 65536 | tf_op jit(solution)/shard_map/while/body/eval_jaxpr/psum | solution.py:72
  733.2 12.4 %bitcast_dynamic-update-slice_fusion.2 = (bf16[4,256,1024]{2,1,0:T(8,128)(2,1)}, bf16[256,1024]{1,0:T(8,128)(2,1)S(1)}) fusion(bf16[4,256,1024]{2,1,0:T(8,128)(2,1)} %get-tuple-element.434, s32[]{:T(128)S(6)} %min.21, bf16[1,256,1024]{2,1,0:T(8,128)(2,1)} %constant_dynamic-slice_fusion.3, pred[]{:T(512)S(6)} %and.44, f32[256,1024]{1,0:T(8,128)S(1)} %bitcast.73, ...), kind=kOutput, calls=%fused_computation.12.clone.1 | convolution fusion | flops 4296278016 | bytes 24117252 | tf_op jit(solution)/shard_map/while/body/eval_jaxpr/dot_general | solution.py:56
  746.4 46.2 %reduce-scatter.2.cloned.1.call-done = bf16[1,256,1024]{2,1,0:T(8,128)(2,1)} async-done(((bf16[4,256,1024]{2,1,0:T(8,128)(2,1)}), bf16[1,256,1024]{2,1,0:T(8,128)(2,1)}) %reduce-scatter.2.cloned.1.call-update) | async-done | bytes 524304 | tf_op jit(solution)/shard_map/reduce_scatter | solution.py:106
  793.8 13.6 %psum.31 = f32[1,256]{1,0:T(1,128)S(1)} all-reduce(f32[1,256]{1,0:T(1,128)S(1)} %bitcast.80), channel_id=1, replica_groups=mesh['section'=4,'mp'=8] {'mp'}, use_global_device_ids=true, to_apply=%region_7.8 | all-reduce | flops 256 | bytes 2048 | tf_op jit(solution)/shard_map/psum | solution.py:115
  (158 shorter events, 219.5 us)
Async XLA Ops:
  7.2 176.0 %all-gather.3.cloned.1.call-start = ((), (), s32[]{:S(2)}) async-start(), calls=%async_computation.3 | async-start | bytes 2621440 | tf_op jit(solution)/shard_map/all_gather | solution.py:37
  65.5 3.9 copy-start.1
  65.5 58.6 %all-to-all-start = ((bf16[8,2,32768]{2,1,0:T(2,128)(2,1)}), bf16[8,2,32768]{2,1,0:T(2,128)(2,1)S(1)}, u32[]{:S(2)}, u32[]{:S(2)}) async-start(bf16[8,2,32768]{2,1,0:T(2,128)(2,1)} %reshape.95), calls=%async_computation | async-start | bytes 2097152 | tf_op jit(solution)/shard_map/all_to_all | solution.py:42
  121.4 6.9 copy-start.2
  121.4 6.9 copy-start.4
  124.1 44.8 %all-to-all-start.1 = ((bf16[8,2,32768]{2,1,0:T(2,128)(2,1)}), bf16[8,2,32768]{2,1,0:T(2,128)(2,1)S(1)}, u32[]{:S(2)}, u32[]{:S(2)}) async-start(bf16[8,2,32768]{2,1,0:T(2,128)(2,1)} %reshape.97), calls=%async_computation.1 | async-start | bytes 2097152 | tf_op jit(solution)/shard_map/all_to_all | solution.py:38
  184.8 68.1 %all-gather.5.cloned.1.call-start = ((), (), s32[]{:S(2)}) async-start(), calls=%async_computation.5 | async-start | bytes 4718592 | tf_op jit(solution)/shard_map/while/body/eval_jaxpr/all_gather | solution.py:57
  184.8 16.2 %collective-permute-start = (bf16[256,1024]{1,0:T(8,128)(2,1)S(1)}, bf16[256,1024]{1,0:T(8,128)(2,1)S(1)}, u32[]{:S(2)}, u32[]{:S(2)}) collective-permute-start(bf16[256,1024]{1,0:T(8,128)(2,1)S(1)} %broadcast_select_fusion.2), channel_id=1, source_target_pairs={{0,8},{8,16},{16,24},{1,9},{9,17},{17,25},{2,10},{10,18},{18,26},{... | collective-permute-start | bytes 1572872 | tf_op jit(solution)/shard_map/while/body/eval_jaxpr/ppermute | solution.py:12
  216.6 4.5 copy-start
  265.3 67.6 %all-gather.5.cloned.1.call-start = ((), (), s32[]{:S(2)}) async-start(), calls=%async_computation.5 | async-start | bytes 4718592 | tf_op jit(solution)/shard_map/while/body/eval_jaxpr/all_gather | solution.py:57
  265.3 16.0 %collective-permute-start = (bf16[256,1024]{1,0:T(8,128)(2,1)S(1)}, bf16[256,1024]{1,0:T(8,128)(2,1)S(1)}, u32[]{:S(2)}, u32[]{:S(2)}) collective-permute-start(bf16[256,1024]{1,0:T(8,128)(2,1)S(1)} %broadcast_select_fusion.2), channel_id=1, source_target_pairs={{0,8},{8,16},{16,24},{1,9},{9,17},{17,25},{2,10},{10,18},{18,26},{... | collective-permute-start | bytes 1572872 | tf_op jit(solution)/shard_map/while/body/eval_jaxpr/ppermute | solution.py:12
  295.9 4.5 copy-start
  345.3 67.7 %all-gather.5.cloned.1.call-start = ((), (), s32[]{:S(2)}) async-start(), calls=%async_computation.5 | async-start | bytes 4718592 | tf_op jit(solution)/shard_map/while/body/eval_jaxpr/all_gather | solution.py:57
  345.3 16.0 %collective-permute-start = (bf16[256,1024]{1,0:T(8,128)(2,1)S(1)}, bf16[256,1024]{1,0:T(8,128)(2,1)S(1)}, u32[]{:S(2)}, u32[]{:S(2)}) collective-permute-start(bf16[256,1024]{1,0:T(8,128)(2,1)S(1)} %broadcast_select_fusion.2), channel_id=1, source_target_pairs={{0,8},{8,16},{16,24},{1,9},{9,17},{17,25},{2,10},{10,18},{18,26},{... | collective-permute-start | bytes 1572872 | tf_op jit(solution)/shard_map/while/body/eval_jaxpr/ppermute | solution.py:12
  376.0 4.5 copy-start
  425.3 67.7 %all-gather.5.cloned.1.call-start = ((), (), s32[]{:S(2)}) async-start(), calls=%async_computation.5 | async-start | bytes 4718592 | tf_op jit(solution)/shard_map/while/body/eval_jaxpr/all_gather | solution.py:57
  425.4 16.0 %collective-permute-start = (bf16[256,1024]{1,0:T(8,128)(2,1)S(1)}, bf16[256,1024]{1,0:T(8,128)(2,1)S(1)}, u32[]{:S(2)}, u32[]{:S(2)}) collective-permute-start(bf16[256,1024]{1,0:T(8,128)(2,1)S(1)} %broadcast_select_fusion.2), channel_id=1, source_target_pairs={{0,8},{8,16},{16,24},{1,9},{9,17},{17,25},{2,10},{10,18},{18,26},{... | collective-permute-start | bytes 1572872 | tf_op jit(solution)/shard_map/while/body/eval_jaxpr/ppermute | solution.py:12
  456.0 4.5 copy-start
  505.4 67.7 %all-gather.5.cloned.1.call-start = ((), (), s32[]{:S(2)}) async-start(), calls=%async_computation.5 | async-start | bytes 4718592 | tf_op jit(solution)/shard_map/while/body/eval_jaxpr/all_gather | solution.py:57
  505.5 16.0 %collective-permute-start = (bf16[256,1024]{1,0:T(8,128)(2,1)S(1)}, bf16[256,1024]{1,0:T(8,128)(2,1)S(1)}, u32[]{:S(2)}, u32[]{:S(2)}) collective-permute-start(bf16[256,1024]{1,0:T(8,128)(2,1)S(1)} %broadcast_select_fusion.2), channel_id=1, source_target_pairs={{0,8},{8,16},{16,24},{1,9},{9,17},{17,25},{2,10},{10,18},{18,26},{... | collective-permute-start | bytes 1572872 | tf_op jit(solution)/shard_map/while/body/eval_jaxpr/ppermute | solution.py:12
  536.1 4.5 copy-start
  585.5 67.7 %all-gather.5.cloned.1.call-start = ((), (), s32[]{:S(2)}) async-start(), calls=%async_computation.5 | async-start | bytes 4718592 | tf_op jit(solution)/shard_map/while/body/eval_jaxpr/all_gather | solution.py:57
  585.5 16.0 %collective-permute-start = (bf16[256,1024]{1,0:T(8,128)(2,1)S(1)}, bf16[256,1024]{1,0:T(8,128)(2,1)S(1)}, u32[]{:S(2)}, u32[]{:S(2)}) collective-permute-start(bf16[256,1024]{1,0:T(8,128)(2,1)S(1)} %broadcast_select_fusion.2), channel_id=1, source_target_pairs={{0,8},{8,16},{16,24},{1,9},{9,17},{17,25},{2,10},{10,18},{18,26},{... | collective-permute-start | bytes 1572872 | tf_op jit(solution)/shard_map/while/body/eval_jaxpr/ppermute | solution.py:12
  616.1 4.5 copy-start
  665.6 67.6 %all-gather.5.cloned.1.call-start = ((), (), s32[]{:S(2)}) async-start(), calls=%async_computation.5 | async-start | bytes 4718592 | tf_op jit(solution)/shard_map/while/body/eval_jaxpr/all_gather | solution.py:57
  665.6 16.0 %collective-permute-start = (bf16[256,1024]{1,0:T(8,128)(2,1)S(1)}, bf16[256,1024]{1,0:T(8,128)(2,1)S(1)}, u32[]{:S(2)}, u32[]{:S(2)}) collective-permute-start(bf16[256,1024]{1,0:T(8,128)(2,1)S(1)} %broadcast_select_fusion.2), channel_id=1, source_target_pairs={{0,8},{8,16},{16,24},{1,9},{9,17},{17,25},{2,10},{10,18},{18,26},{... | collective-permute-start | bytes 1572872 | tf_op jit(solution)/shard_map/while/body/eval_jaxpr/ppermute | solution.py:12
  696.2 4.5 copy-start
  745.6 0.7 copy-start.3
  745.6 61.8 %copy-start.5 = (s32[1,2]{1,0:T(1,128)S(1)}, s32[1,2]{1,0:T(1,128)}, u32[]{:S(2)}) copy-start(s32[1,2]{1,0:T(1,128)} %param.17) | copy-start | bytes 28
  745.6 46.9 %reduce-scatter.2.cloned.1.call-start = ((), (), s32[]{:S(2)}) async-start(), calls=%async_computation.4 | async-start | bytes 2621440 | tf_op jit(solution)/shard_map/reduce_scatter | solution.py:106
Sparse Core Ops, SparseCore 0:
  9.6 45.6 all-gather.2
  216.7 36.0 all-gather.4
  296.0 36.8 all-gather.4
  376.1 36.8 all-gather.4
  456.1 36.8 all-gather.4
  536.2 36.8 all-gather.4
  616.2 36.8 all-gather.4
  696.3 36.8 all-gather.4
  749.3 43.1 reduce-scatter.1
where the time goes:
time: 819 us; the launch traced here: 815 us
  blocking collectives  260 us (32%)
  waiting for transfers between devices  198 us (24%)
  other arithmetic  109 us (13%)
  matrix products  107 us (13%)
  local copies, waits for them, and re-layouts  94 us (11%)
  starting transfers between devices  31.9 us (4%)
  between operations  13.9 us (2%)
    psum x7, blocking collectives, layer_of_section(): lax.psum(compressed_projection.astype(jnp.bfloat16), 'mp')  160 us
    unnamed x3, other arithmetic  90.4 us
    ppermute x7, waiting for transfers between devices, shifted(): lax.ppermute(value, axis, [(source, source + steps) for source in range(i...  88.1 us
    psum x7, blocking collectives, layer_of_section(): squares = lax.psum(jnp.sum(hidden_f * hidden_f, axis=1), 'mp')  87 us
    dot_general x7, matrix products, layer_of_section(): jnp.dot(lax.all_gather(rescaled_activation, 'mp', axis=1, tiled=True), we...  86.8 us
    all_gather x7, waiting for transfers between devices, layer_of_section(): lax.all_gather(rescaled_activation, 'mp', axis=1, tiled=True)  62.4 us
    reduce_scatter x1, waiting for transfers between devices, shards(): lax.psum_scatter(finished.astype(jnp.float32).astype(jnp.bfloat16), 'sect...  46.2 us
    all_to_all x1, local copies, waits for them, and re-layouts, shards(): lax.all_to_all(plugin_narrowing_factors, 'mp', split_axis=2, concat_axis=...  33.1 us
  transfers between devices with their start and end apart: 18, of which 15 were waited for; matrix products, arithmetic and copies ran while one was open for 25% of the time, Pallas kernels for 0%

commit v1 on v0

v1 whole, which is shorter than its diff:
```python
import functools

import jax
import jax.numpy as jnp
from jax import lax
from jax.experimental import pallas as pl
from jax.experimental.pallas import tpu as pltpu
from jax.sharding import PartitionSpec as P

BLOCK = 128
SIDE = 128
LAG = 2
GATHER = "ag"


def prep_kernel(rank, s_ref, *refs):
    *sources, gain_ref, table_ref, x_ref, m_ref = refs
    copies, _, _ = m_ref.shape
    piece = x_ref.shape[1]
    if len(sources) == 2:
        x = jnp.where(s_ref[1] == 0, sources[0][...].astype(jnp.float32), sources[1][...].astype(jnp.float32))
    else:
        x = sources[0][...].astype(jnp.float32)
    x_ref[...] = x.astype(jnp.bfloat16)
    scaled = (x * gain_ref[...].astype(jnp.float32)).astype(jnp.bfloat16)
    squares = jnp.sum(x * x, axis=1, keepdims=True)
    high = squares.astype(jnp.bfloat16).astype(jnp.float32)
    low = squares - high
    inner = lax.dot_general(
        scaled, table_ref[0], (((1,), (1,)), ((), ())), preferred_element_type=jnp.float32
    )
    lane = lax.broadcasted_iota(jnp.int32, inner.shape, 1)
    side = jnp.where(lane < rank, inner, jnp.where(lane == rank, high, jnp.where(lane == rank + 1, low, 0.0)))
    side = side[:, :SIDE].astype(jnp.bfloat16)
    for copy in range(copies):
        m_ref[copy, :, :piece] = scaled
        m_ref[copy, :, piece:] = side


def prep(scalars, sources, block, gain, table, rank, copies):
    piece = gain.shape[1]
    rows = BLOCK
    specs = [
        pl.BlockSpec((rows, piece), functools.partial(lambda b, i, s: (b, 0), b))
        for b in block
    ]
    return pl.pallas_call(
        functools.partial(prep_kernel, rank),
        out_shape=(
            jax.ShapeDtypeStruct((rows, piece), jnp.bfloat16),
            jax.ShapeDtypeStruct((copies, rows, piece + SIDE), jnp.bfloat16),
        ),
        grid_spec=pltpu.PrefetchScalarGridSpec(
            num_scalar_prefetch=1,
            grid=(1,),
            in_specs=specs
            + [
                pl.BlockSpec((1, piece), lambda i, s: (0, 0)),
                pl.BlockSpec((1,) + table.shape[1:], lambda i, s: (s[0], 0, 0)),
            ],
            out_specs=(
                pl.BlockSpec((rows, piece), lambda i, s: (0, 0)),
                pl.BlockSpec((copies, rows, piece + SIDE), lambda i, s: (0, 0, 0)),
            ),
        ),
        cost_estimate=pl.CostEstimate(
            flops=2 * rows * piece * SIDE, bytes_accessed=rows * piece * 8, transcendentals=0
        ),
        name="prep",
    )(scalars, *sources, gain, table)


def layer_kernel(rank, width, counts, s_ref, *refs):
    *parts, w_ref, x_ref, table_ref, o_ref, total, side = refs
    step = pl.program_id(0)
    piece = o_ref.shape[1]

    @pl.when(step == 0)
    def _():
        total[...] = jnp.zeros_like(total)
        side[...] = jnp.zeros_like(side)

    start = 0
    for part, count in zip(parts, counts):
        @pl.when((step >= start) & (step < start + count))
        def _():
            total[...] += jnp.dot(part[0, :, :piece], w_ref[...], preferred_element_type=jnp.float32)
            side[...] += part[0, :, piece:].astype(jnp.float32)

        start += count

    @pl.when(step == start - 1)
    def _():
        squares = side[:, rank : rank + 1] + side[:, rank + 1 : rank + 2]
        scale = lax.rsqrt(squares / width + 1e-05)
        inner = side[:, :rank].astype(jnp.bfloat16)
        delta = jnp.dot(inner, table_ref[0, rank : 2 * rank, :], preferred_element_type=jnp.float32)
        h = x_ref[...].astype(jnp.float32)
        o_ref[...] = (h + scale * (total[...] + 2.0 * delta)).astype(jnp.bfloat16)


def layer(scalars, parts, weight, x, table, rank):
    rows, piece = x.shape
    width = weight.shape[0]
    counts = tuple(part.shape[0] for part in parts)
    owners = sum(counts)
    part_specs = []
    start = 0
    for count in counts:
        part_specs.append(
            pl.BlockSpec(
                (1, rows, piece + SIDE),
                functools.partial(lambda a, c, i, s: (jnp.clip(i - a, 0, c - 1), 0, 0), start, count),
            )
        )
        start += count
    return pl.pallas_call(
        functools.partial(layer_kernel, rank, width, counts),
        out_shape=jax.ShapeDtypeStruct((rows, piece), jnp.bfloat16),
        grid_spec=pltpu.PrefetchScalarGridSpec(
            num_scalar_prefetch=1,
            grid=(owners,),
            in_specs=part_specs
            + [
                pl.BlockSpec((piece, piece), lambda i, s: (s[2 + i], 0)),
                pl.BlockSpec((rows, piece), lambda i, s: (0, 0)),
                pl.BlockSpec((1,) + table.shape[1:], lambda i, s: (s[0], 0, 0)),
            ],
            out_specs=pl.BlockSpec((rows, piece), lambda i, s: (0, 0)),
            scratch_shapes=[
                pltpu.VMEM((rows, piece), jnp.float32),
                pltpu.VMEM((rows, SIDE), jnp.float32),
            ],
        ),
        cost_estimate=pl.CostEstimate(
            flops=2 * rows * width * piece, bytes_accessed=2 * width * piece, transcendentals=0
        ),
        name="layer",
    )(scalars, *parts, weight, x, table)


def shards(
    entering_hidden,
    section_weight,
    section_norm_gain,
    plugin_narrowing_factors,
    plugin_widening_factors,
    reward_head,
    adapter_of_block,
    live_block_rows,
):
    sections = lax.axis_size("section")
    section = lax.axis_index("section")
    chips = lax.axis_size("chip")
    cores = lax.axis_size("core")
    owners = chips * cores
    everyone = ("chip", "core")
    me = lax.axis_index(everyone)
    batches_here, rows, piece = entering_hidden.shape
    micro = batches_here * sections
    per_micro = rows // BLOCK
    owned = plugin_narrowing_factors.shape[1]
    rank = plugin_narrowing_factors.shape[3]
    weight = section_weight[0]
    chunks = micro * per_micro

    down = jnp.swapaxes(plugin_narrowing_factors[0], 1, 2)
    maps = jnp.concatenate([down, plugin_widening_factors[0]], axis=1)
    maps = jnp.moveaxis(maps.reshape(owned, 2 * rank, owners, piece), 2, 0)
    table = lax.all_to_all(maps, everyone, split_axis=0, concat_axis=0, tiled=True)
    table = table.reshape(owners * owned, 2 * rank, piece)

    feeds = []
    for m in range(micro):
        home, slot = divmod(m, batches_here)
        block = entering_hidden[slot]
        feeds.append(block if home == 0 else lax.ppermute(block, "section", [(home, 0)]))

    adapters = adapter_of_block.reshape(-1)
    if GATHER == "ag":
        order = jnp.arange(owners, dtype=jnp.int32)
        copies = 1
    else:
        chip, core = lax.axis_index("chip"), lax.axis_index("core")
        base = jnp.arange(chips, dtype=jnp.int32) * cores
        order = jnp.concatenate([base + (core + k) % cores for k in range(cores)])
        copies = chips

    def gathered(message):
        if GATHER == "ag":
            return [lax.all_gather(message, everyone, axis=0, tiled=True)]
        parts = lax.all_to_all(message, "chip", split_axis=0, concat_axis=0, tiled=True)
        out = [parts]
        for k in range(1, cores):
            out.append(lax.ppermute(parts, "core", [((c + k) % cores, c) for c in range(cores)]))
        return out

    arrived = {}
    done = {}
    zero = jnp.zeros((BLOCK, piece), jnp.bfloat16)
    for tick in range(chunks + LAG * (sections - 1)):
        active = [s for s in range(sections) if 0 <= tick - LAG * s < chunks]
        mine = jnp.clip(tick - LAG * section, 0, chunks - 1)
        adapter = lax.dynamic_index_in_dim(adapters, mine, 0, keepdims=True)
        scalars = jnp.concatenate([adapter, section[None].astype(jnp.int32), order])
        sources, blocks = [], []
        if 0 in active:
            m, b = divmod(tick, per_micro)
            sources.append(feeds[m])
            blocks.append(b)
        if active != [0]:
            sources.append(arrived.pop(tick, zero))
            blocks.append(0)
        x, message = prep(scalars, sources, blocks, section_norm_gain, table, rank, copies)
        parts = gathered(message)
        h = layer(scalars, parts, weight, x, table, rank)
        onward = [(s, s + 1) for s in active if s + 1 < sections]
        if onward:
            arrived[tick + LAG] = lax.ppermute(h, "section", onward)
        if sections - 1 in active:
            done[tick - LAG * (sections - 1)] = h

    slots = []
    for slot in range(batches_here):
        value = None
        for home in range(sections):
            m = home * batches_here + slot
            block = jnp.concatenate([done[m * per_micro + b] for b in range(per_micro)], axis=0)
            if home != sections - 1:
                block = lax.ppermute(block, "section", [(sections - 1, home)])
            value = block if value is None else jnp.where(section == home, block, value)
        slots.append(value)
    hidden_out = jnp.stack(slots)
    partial_score = jnp.sum(
        hidden_out.astype(jnp.float32) * reward_head.astype(jnp.float32)[None, None, :], axis=2
    )
    raw = lax.psum(partial_score, everyone)
    place = jnp.arange(rows, dtype=jnp.int32) % BLOCK
    limits = jnp.repeat(live_block_rows, BLOCK, axis=1)
    scores = jnp.where(place[None, :] < limits, raw, jnp.float32(0.0))
    return (hidden_out, scores)


def solution(mesh):
    sections, owners = mesh.shape["section"], mesh.shape["mp"]
    cores = 2 if owners % 2 == 0 else 1
    fine = jax.sharding.Mesh(
        mesh.devices.reshape(sections, owners // cores, cores), ("section", "chip", "core")
    )
    mp = ("chip", "core")
    placed = (
        P("section", None, mp),
        P("section", None, mp),
        P("section", mp),
        P("section", mp, None, None),
        P("section", mp, None, None),
        P(mp),
        P(),
        P("section", None),
    )
    return jax.shard_map(
        shards,
        mesh=fine,
        in_specs=placed,
        out_specs=(P("section", None, mp), P("section", None)),
        check_vma=False,
    )
```

time: 819 us -> 516 us (0.63)
  blocking collectives: 260 us -> 13.1 us
  Pallas kernels: 0 us -> 203 us
  matrix products: 107 us -> 0 us
  other arithmetic: 109 us -> 15.9 us
  local copies, waits for them, and re-layouts: 94 us -> 15.9 us
  starting transfers between devices: 31.9 us -> 51.2 us
    psum x15 -> x1, blocking collectives: 260 us -> 13.1 us  [shards(): raw = lax.psum(partial_score, everyone)]
    pallas_call x0 -> x28, Pallas kernels: none -> 203 us  [the longest x14 165 us: layer(): pl.pallas_call(functools.partial(layer_kernel, rank, width, counts), out_...]
    dot_general x35 -> x0, matrix products: 107 us -> none  [the longest x7 86.8 us: layer_of_section(): jnp.dot(lax.all_gather(rescaled_activation, 'mp', axis=1, tiled=True), we...]
    unnamed x3 -> x0, other arithmetic: 90.4 us -> none
    reduce_scatter x1 -> x0, waiting for transfers between devices: 46.2 us -> none  [shards(): lax.psum_scatter(finished.astype(jnp.float32).astype(jnp.bfloat16), 'sect...]
    all_gather x8 -> x14, waiting for transfers between devices: 62.4 us -> 106 us  [gathered(): return [lax.all_gather(message, everyone, axis=0, tiled=True)]]
    all_to_all x2 -> x0, local copies, waits for them, and re-layouts: 41.3 us -> none  [the longest x1 33.1 us: shards(): lax.all_to_all(plugin_narrowing_factors, 'mp', split_axis=2, concat_axis=...]
    all_to_all x2 -> x1, waiting for transfers between devices: 0.01 us -> 23.2 us  [shards(): lax.all_to_all(maps, everyone, split_axis=0, concat_axis=0, tiled=True)]
  transfers between devices with their start and end apart: 18 -> 33, of which waited for: 15 -> 25; matrix products, arithmetic and copies ran while one was open for 25% -> 3% of each run, Pallas kernels for 0% -> 39%
where the time goes in v1:
time: 516 us; the launch traced here: 512 us
  Pallas kernels  203 us (39%)
  waiting for transfers between devices  198 us (38%)
  starting transfers between devices  51.2 us (10%)
  local copies, waits for them, and re-layouts  15.9 us (3%)
  other arithmetic  15.9 us (3%)
  between operations  14.4 us (3%)
  blocking collectives  13.1 us (3%)
    pallas_call x14, Pallas kernels, layer(): pl.pallas_call(functools.partial(layer_kernel, rank, width, counts), out_...  165 us
    all_gather x14, waiting for transfers between devices, gathered(): return [lax.all_gather(message, everyone, axis=0, tiled=True)]  106 us
    ppermute x12, waiting for transfers between devices, shards(): arrived[tick + LAG] = lax.ppermute(h, 'section', onward)  68.8 us
    pallas_call x14, Pallas kernels, prep(): pl.pallas_call(functools.partial(prep_kernel, rank), out_shape=(jax.Shape...  38.3 us
    ppermute x12, starting transfers between devices, shards(): arrived[tick + LAG] = lax.ppermute(h, 'section', onward)  31.3 us
    all_to_all x1, waiting for transfers between devices, shards(): lax.all_to_all(maps, everyone, split_axis=0, concat_axis=0, tiled=True)  23.2 us
    psum x1, blocking collectives, shards(): raw = lax.psum(partial_score, everyone)  13.1 us
    ppermute x3, starting transfers between devices, shards(): lax.ppermute(block, 'section', [(home, 0)])  12.8 us
  transfers between devices with their start and end apart: 33, of which 25 were waited for; matrix products, arithmetic and copies ran while one was open for 3% of the time, Pallas kernels for 39%

profile of v1, /device:TPU:16, one launch (start us, length us, event | category | flops | bytes accessed | tf_op | source)
XLA Modules:
  0.0 512.2 jit_solution(7786893525564412796)
XLA Ops:
  19.7 23.2 %all-to-all-done = bf16[8,1,128,1024]{3,2,1,0:T(8,128)(2,1)S(1)} async-done(((bf16[8,1,128,1024]{3,2,1,0:T(8,128)(2,1)}), bf16[8,1,128,1024]{3,2,1,0:T(8,128)(2,1)S(1)}, u32[]{:S(2)}, u32[]{:S(2)}) %all-to-all-start) | async-done | bytes 2097184 | tf_op jit(solution)/shard_map/all_to_all | solution.py:170
  53.2 22.3 %all-gather.29.cloned.1.call-done.refs_0_ = bf16[8,128,1152]{2,1,0:T(8,128)(2,1)} async-done(((bf16[1,128,1152]{2,1,0:T(8,128)(2,1)}), bf16[8,128,1152]{2,1,0:T(8,128)(2,1)}) %all-gather.29.cloned.1.call-update) | async-done | bytes 2359312 | tf_op jit(solution)/shard_map/all_gather | solution.py:191
  75.5 11.8 %layer.21 = bf16[128,1024]{1,0:T(8,128)(2,1)} custom-call(s32[10]{0:T(128)} %get-tuple-element.83.s_ref, bf16[8,128,1152]{2,1,0:T(8,128)(2,1)} %all-gather.29.cloned.1.call-done.refs_0_, bf16[8192,1024]{1,0:T(8,128)(2,1)} %bitcast.22, bf16[128,1024]{1,0:T(8,128)(2,1)} %get-tuple-element.45.refs_2_, bf16[8,128,1024]{2,1,0:T(8,128)(2,1)} %bitcast.38), custom_call_target="tpu_custom_call" | custom-call | flops 2147483648 | bytes 16777216 | tf_op jit(solution)/shard_map/layer/pallas_call | solution.py:117
  93.6 12.8 %all-gather.15.cloned.1.call-done.refs_0_ = bf16[8,128,1152]{2,1,0:T(8,128)(2,1)} async-done(((bf16[1,128,1152]{2,1,0:T(8,128)(2,1)}), bf16[8,128,1152]{2,1,0:T(8,128)(2,1)}) %all-gather.15.cloned.1.call-update) | async-done | bytes 2359312 | tf_op jit(solution)/shard_map/all_gather | solution.py:191
  106.4 11.8 %layer.14 = bf16[128,1024]{1,0:T(8,128)(2,1)} custom-call(s32[10]{0:T(128)} %get-tuple-element.80.s_ref, bf16[8,128,1152]{2,1,0:T(8,128)(2,1)} %all-gather.15.cloned.1.call-done.refs_0_, bf16[8192,1024]{1,0:T(8,128)(2,1)} %bitcast.23, bf16[128,1024]{1,0:T(8,128)(2,1)} %get-tuple-element.31.refs_2_, bf16[8,128,1024]{2,1,0:T(8,128)(2,1)} %bitcast.40), custom_call_target="tpu_custom_call" | custom-call | flops 2147483648 | bytes 16777216 | tf_op jit(solution)/shard_map/layer/pallas_call | solution.py:117
  122.5 11.4 %collective-permute-start.1 = (bf16[256,1024]{1,0:T(8,128)(2,1)S(1)}, bf16[256,1024]{1,0:T(8,128)(2,1)S(1)}, u32[]{:S(2)}, u32[]{:S(2)}) collective-permute-start(bf16[256,1024]{1,0:T(8,128)(2,1)S(1)} %bitcast.69), channel_id=1, source_target_pairs={{16,0},{17,1},{18,2},{19,3},{20,4},{21,5},{22,6},{23,7}} | collective-permute-start | bytes 1572872 | tf_op jit(solution)/shard_map/ppermute | solution.py:177
  137.4 11.8 %layer.22 = bf16[128,1024]{1,0:T(8,128)(2,1)} custom-call(s32[10]{0:T(128)} %get-tuple-element.86.s_ref, bf16[8,128,1152]{2,1,0:T(8,128)(2,1)} %all-gather.31.cloned.1.call-done.refs_0_, bf16[8192,1024]{1,0:T(8,128)(2,1)} %bitcast.24, bf16[128,1024]{1,0:T(8,128)(2,1)} %get-tuple-element.47.refs_2_, bf16[8,128,1024]{2,1,0:T(8,128)(2,1)} %bitcast.42), custom_call_target="tpu_custom_call" | custom-call | flops 2147483648 | bytes 16777216 | tf_op jit(solution)/shard_map/layer/pallas_call | solution.py:117
  150.5 9.2 %collective-permute-done.10.refs_1_ = bf16[128,1024]{1,0:T(8,128)(2,1)S(1)} collective-permute-done((bf16[128,1024]{1,0:T(8,128)(2,1)}, bf16[128,1024]{1,0:T(8,128)(2,1)S(1)}, u32[]{:S(2)}, u32[]{:S(2)}) %collective-permute-start.10) | collective-permute-done | bytes 262176 | tf_op jit(solution)/shard_map/ppermute | solution.py:219
  168.2 11.8 %layer.15 = bf16[128,1024]{1,0:T(8,128)(2,1)} custom-call(s32[10]{0:T(128)} %get-tuple-element.81.s_ref, bf16[8,128,1152]{2,1,0:T(8,128)(2,1)} %all-gather.17.cloned.1.call-done.refs_0_, bf16[8192,1024]{1,0:T(8,128)(2,1)} %bitcast.25, bf16[128,1024]{1,0:T(8,128)(2,1)} %get-tuple-element.33.refs_2_, bf16[8,128,1024]{2,1,0:T(8,128)(2,1)} %bitcast.44), custom_call_target="tpu_custom_call" | custom-call | flops 2147483648 | bytes 16777216 | tf_op jit(solution)/shard_map/layer/pallas_call | solution.py:117
  183.8 6.7 %collective-permute-done.4.refs_1_ = bf16[128,1024]{1,0:T(8,128)(2,1)S(1)} collective-permute-done((bf16[128,1024]{1,0:T(8,128)(2,1)}, bf16[128,1024]{1,0:T(8,128)(2,1)S(1)}, u32[]{:S(2)}, u32[]{:S(2)}) %collective-permute-start.4) | collective-permute-done | bytes 262176 | tf_op jit(solution)/shard_map/ppermute | solution.py:219
  199.0 11.8 %layer.23 = bf16[128,1024]{1,0:T(8,128)(2,1)} custom-call(s32[10]{0:T(128)} %get-tuple-element.87.s_ref, bf16[8,128,1152]{2,1,0:T(8,128)(2,1)} %all-gather.33.cloned.1.call-done.refs_0_, bf16[8192,1024]{1,0:T(8,128)(2,1)} %bitcast.26, bf16[128,1024]{1,0:T(8,128)(2,1)} %get-tuple-element.49.refs_2_, bf16[8,128,1024]{2,1,0:T(8,128)(2,1)} %bitcast.46), custom_call_target="tpu_custom_call" | custom-call | flops 2147483648 | bytes 16777216 | tf_op jit(solution)/shard_map/layer/pallas_call | solution.py:117
  214.2 7.1 %collective-permute-done.11.refs_1_ = bf16[128,1024]{1,0:T(8,128)(2,1)S(1)} collective-permute-done((bf16[128,1024]{1,0:T(8,128)(2,1)}, bf16[128,1024]{1,0:T(8,128)(2,1)S(1)}, u32[]{:S(2)}, u32[]{:S(2)}) %collective-permute-start.11) | collective-permute-done | bytes 262176 | tf_op jit(solution)/shard_map/ppermute | solution.py:219
  229.8 11.8 %layer.16 = bf16[128,1024]{1,0:T(8,128)(2,1)} custom-call(s32[10]{0:T(128)} %get-tuple-element.79.s_ref, bf16[8,128,1152]{2,1,0:T(8,128)(2,1)} %all-gather.19.cloned.1.call-done.refs_0_, bf16[8192,1024]{1,0:T(8,128)(2,1)} %bitcast.27, bf16[128,1024]{1,0:T(8,128)(2,1)} %get-tuple-element.35.refs_2_, bf16[8,128,1024]{2,1,0:T(8,128)(2,1)} %bitcast.48), custom_call_target="tpu_custom_call" | custom-call | flops 2147483648 | bytes 16777216 | tf_op jit(solution)/shard_map/layer/pallas_call | solution.py:117
  244.9 7.2 %collective-permute-done.5.refs_1_ = bf16[128,1024]{1,0:T(8,128)(2,1)S(1)} collective-permute-done((bf16[128,1024]{1,0:T(8,128)(2,1)}, bf16[128,1024]{1,0:T(8,128)(2,1)S(1)}, u32[]{:S(2)}, u32[]{:S(2)}) %collective-permute-start.5) | collective-permute-done | bytes 262176 | tf_op jit(solution)/shard_map/ppermute | solution.py:219
  260.7 11.8 %layer.24 = bf16[128,1024]{1,0:T(8,128)(2,1)} custom-call(s32[10]{0:T(128)} %get-tuple-element.85.s_ref, bf16[8,128,1152]{2,1,0:T(8,128)(2,1)} %all-gather.35.cloned.1.call-done.refs_0_, bf16[8192,1024]{1,0:T(8,128)(2,1)} %bitcast.28, bf16[128,1024]{1,0:T(8,128)(2,1)} %get-tuple-element.51.refs_2_, bf16[8,128,1024]{2,1,0:T(8,128)(2,1)} %bitcast.50), custom_call_target="tpu_custom_call" | custom-call | flops 2147483648 | bytes 16777216 | tf_op jit(solution)/shard_map/layer/pallas_call | solution.py:117
  275.9 7.2 %collective-permute-done.12.refs_0_ = bf16[128,1024]{1,0:T(8,128)(2,1)S(1)} collective-permute-done((bf16[128,1024]{1,0:T(8,128)(2,1)}, bf16[128,1024]{1,0:T(8,128)(2,1)S(1)}, u32[]{:S(2)}, u32[]{:S(2)}) %collective-permute-start.12) | collective-permute-done | bytes 262176 | tf_op jit(solution)/shard_map/ppermute | solution.py:219
  291.6 11.8 %layer.17 = bf16[128,1024]{1,0:T(8,128)(2,1)} custom-call(s32[10]{0:T(128)} %get-tuple-element.78.s_ref, bf16[8,128,1152]{2,1,0:T(8,128)(2,1)} %all-gather.21.cloned.1.call-done.refs_0_, bf16[8192,1024]{1,0:T(8,128)(2,1)} %bitcast.29, bf16[128,1024]{1,0:T(8,128)(2,1)} %get-tuple-element.37.refs_2_, bf16[8,128,1024]{2,1,0:T(8,128)(2,1)} %bitcast.52), custom_call_target="tpu_custom_call" | custom-call | flops 2147483648 | bytes 16777216 | tf_op jit(solution)/shard_map/layer/pallas_call | solution.py:117
  317.4 5.7 %all-gather.37.cloned.1.call-done.refs_0_ = bf16[8,128,1152]{2,1,0:T(8,128)(2,1)} async-done(((bf16[1,128,1152]{2,1,0:T(8,128)(2,1)}), bf16[8,128,1152]{2,1,0:T(8,128)(2,1)}) %all-gather.37.cloned.1.call-update) | async-done | bytes 2359312 | tf_op jit(solution)/shard_map/all_gather | solution.py:191
  323.2 11.8 %layer.25 = bf16[128,1024]{1,0:T(8,128)(2,1)} custom-call(s32[10]{0:T(128)} %get-tuple-element.84.s_ref, bf16[8,128,1152]{2,1,0:T(8,128)(2,1)} %all-gather.37.cloned.1.call-done.refs_0_, bf16[8192,1024]{1,0:T(8,128)(2,1)} %bitcast.30, bf16[128,1024]{1,0:T(8,128)(2,1)} %get-tuple-element.53.refs_2_, bf16[8,128,1024]{2,1,0:T(8,128)(2,1)} %bitcast.54), custom_call_target="tpu_custom_call" | custom-call | flops 2147483648 | bytes 16777216 | tf_op jit(solution)/shard_map/layer/pallas_call | solution.py:117
  338.3 7.2 %collective-permute-done.13.refs_0_ = bf16[128,1024]{1,0:T(8,128)(2,1)S(1)} collective-permute-done((bf16[128,1024]{1,0:T(8,128)(2,1)}, bf16[128,1024]{1,0:T(8,128)(2,1)S(1)}, u32[]{:S(2)}, u32[]{:S(2)}) %collective-permute-start.13) | collective-permute-done | bytes 262176 | tf_op jit(solution)/shard_map/ppermute | solution.py:219
  353.9 11.8 %layer.18 = bf16[128,1024]{1,0:T(8,128)(2,1)} custom-call(s32[10]{0:T(128)} %get-tuple-element.62.s_ref, bf16[8,128,1152]{2,1,0:T(8,128)(2,1)} %all-gather.23.cloned.1.call-done.refs_0_, bf16[8192,1024]{1,0:T(8,128)(2,1)} %bitcast.31, bf16[128,1024]{1,0:T(8,128)(2,1)} %get-tuple-element.39.refs_2_, bf16[8,128,1024]{2,1,0:T(8,128)(2,1)} %bitcast.56), custom_call_target="tpu_custom_call" | custom-call | flops 2147483648 | bytes 16777216 | tf_op jit(solution)/shard_map/layer/pallas_call | solution.py:117
  369.1 7.2 %collective-permute-done.7.refs_0_ = bf16[128,1024]{1,0:T(8,128)(2,1)S(1)} collective-permute-done((bf16[128,1024]{1,0:T(8,128)(2,1)}, bf16[128,1024]{1,0:T(8,128)(2,1)S(1)}, u32[]{:S(2)}, u32[]{:S(2)}) %collective-permute-start.7) | collective-permute-done | bytes 262176 | tf_op jit(solution)/shard_map/ppermute | solution.py:219
  379.7 5.7 %all-gather.39.cloned.1.call-done.refs_0_ = bf16[8,128,1152]{2,1,0:T(8,128)(2,1)} async-done(((bf16[1,128,1152]{2,1,0:T(8,128)(2,1)}), bf16[8,128,1152]{2,1,0:T(8,128)(2,1)}) %all-gather.39.cloned.1.call-update) | async-done | bytes 2359312 | tf_op jit(solution)/shard_map/all_gather | solution.py:191
  385.5 11.8 %layer.26 = bf16[128,1024]{1,0:T(8,128)(2,1)} custom-call(s32[10]{0:T(128)} %get-tuple-element.82.s_ref, bf16[8,128,1152]{2,1,0:T(8,128)(2,1)} %all-gather.39.cloned.1.call-done.refs_0_, bf16[8192,1024]{1,0:T(8,128)(2,1)} %bitcast.32, bf16[128,1024]{1,0:T(8,128)(2,1)} %get-tuple-element.55.refs_2_, bf16[8,128,1024]{2,1,0:T(8,128)(2,1)} %bitcast.58), custom_call_target="tpu_custom_call" | custom-call | flops 2147483648 | bytes 16777216 | tf_op jit(solution)/shard_map/layer/pallas_call | solution.py:117
  400.6 6.3 %collective-permute-done.14.refs_0_ = bf16[128,1024]{1,0:T(8,128)(2,1)S(1)} collective-permute-done((bf16[128,1024]{1,0:T(8,128)(2,1)}, bf16[128,1024]{1,0:T(8,128)(2,1)S(1)}, u32[]{:S(2)}, u32[]{:S(2)}) %collective-permute-start.14) | collective-permute-done | bytes 262176 | tf_op jit(solution)/shard_map/ppermute | solution.py:219
  410.4 5.9 %all-gather.25.cloned.1.call-done.refs_0_ = bf16[8,128,1152]{2,1,0:T(8,128)(2,1)} async-done(((bf16[1,128,1152]{2,1,0:T(8,128)(2,1)}), bf16[8,128,1152]{2,1,0:T(8,128)(2,1)}) %all-gather.25.cloned.1.call-update) | async-done | bytes 2359312 | tf_op jit(solution)/shard_map/all_gather | solution.py:191
  416.2 11.8 %layer.19 = bf16[128,1024]{1,0:T(8,128)(2,1)} custom-call(s32[10]{0:T(128)} %get-tuple-element.61.s_ref, bf16[8,128,1152]{2,1,0:T(8,128)(2,1)} %all-gather.25.cloned.1.call-done.refs_0_, bf16[8192,1024]{1,0:T(8,128)(2,1)} %bitcast.33, bf16[128,1024]{1,0:T(8,128)(2,1)} %get-tuple-element.41.refs_2_, bf16[8,128,1024]{2,1,0:T(8,128)(2,1)} %bitcast.60), custom_call_target="tpu_custom_call" | custom-call | flops 2147483648 | bytes 16777216 | tf_op jit(solution)/shard_map/layer/pallas_call | solution.py:117
  431.6 6.3 %collective-permute-done.8.refs_0_ = bf16[128,1024]{1,0:T(8,128)(2,1)S(1)} collective-permute-done((bf16[128,1024]{1,0:T(8,128)(2,1)}, bf16[128,1024]{1,0:T(8,128)(2,1)S(1)}, u32[]{:S(2)}, u32[]{:S(2)}) %collective-permute-start.8) | collective-permute-done | bytes 262176 | tf_op jit(solution)/shard_map/ppermute | solution.py:219
  447.2 11.8 %layer.27 = bf16[128,1024]{1,0:T(8,128)(2,1)} custom-call(s32[10]{0:T(128)} %get-tuple-element.77.s_ref, bf16[8,128,1152]{2,1,0:T(8,128)(2,1)} %all-gather.41.cloned.1.call-done.refs_0_, bf16[8192,1024]{1,0:T(8,128)(2,1)} %bitcast.34, bf16[128,1024]{1,0:T(8,128)(2,1)} %get-tuple-element.57.refs_2_, bf16[8,128,1024]{2,1,0:T(8,128)(2,1)} %bitcast.62), custom_call_target="tpu_custom_call" | custom-call | flops 2147483648 | bytes 16777216 | tf_op jit(solution)/shard_map/layer/pallas_call | solution.py:117
  459.0 19.0 %all-gather.27.cloned.1.call-done.refs_0_ = bf16[8,128,1152]{2,1,0:T(8,128)(2,1)} async-done(((bf16[1,128,1152]{2,1,0:T(8,128)(2,1)}), bf16[8,128,1152]{2,1,0:T(8,128)(2,1)}) %all-gather.27.cloned.1.call-update) | async-done | bytes 2359312 | tf_op jit(solution)/shard_map/all_gather | solution.py:191
  478.0 11.8 %layer.20 = bf16[128,1024]{1,0:T(8,128)(2,1)} custom-call(s32[10]{0:T(128)} %get-tuple-element.60.s_ref, bf16[8,128,1152]{2,1,0:T(8,128)(2,1)} %all-gather.27.cloned.1.call-done.refs_0_, bf16[8192,1024]{1,0:T(8,128)(2,1)} %bitcast.35, bf16[128,1024]{1,0:T(8,128)(2,1)} %get-tuple-element.43.refs_2_, bf16[8,128,1024]{2,1,0:T(8,128)(2,1)} %bitcast.63), custom_call_target="tpu_custom_call" | custom-call | flops 2147483648 | bytes 16777216 | tf_op jit(solution)/shard_map/layer/pallas_call | solution.py:117
  491.9 13.1 %psum.7 = f32[1,256]{1,0:T(1,128)S(1)} all-reduce(f32[1,256]{1,0:T(1,128)S(1)} %bitcast.74), channel_id=1, replica_groups=mesh['section'=4,'chip'=4,'core'=2] {'chip','core'}, use_global_device_ids=true, to_apply=%region_1.2 | all-reduce | flops 256 | bytes 2048 | tf_op jit(solution)/shard_map/psum | solution.py:237
  (153 shorter events, 149.2 us)
Async XLA Ops:
  12.4 30.5 %all-to-all-start = ((bf16[8,1,128,1024]{3,2,1,0:T(8,128)(2,1)}), bf16[8,1,128,1024]{3,2,1,0:T(8,128)(2,1)S(1)}, u32[]{:S(2)}, u32[]{:S(2)}) async-start(bf16[8,1,128,1024]{3,2,1,0:T(8,128)(2,1)} %copy.15), calls=%async_computation | async-start | bytes 4194304 | tf_op jit(solution)/shard_map/all_to_all | solution.py:170
  16.2 59.3 %all-gather.29.cloned.1.call-start = ((), (), s32[]{:S(2)}) async-start(), calls=%async_computation.8 | async-start | bytes 2654208 | tf_op jit(solution)/shard_map/all_gather | solution.py:191
  47.1 59.3 %all-gather.15.cloned.1.call-start = ((), (), s32[]{:S(2)}) async-start(), calls=%async_computation.1 | async-start | bytes 2654208 | tf_op jit(solution)/shard_map/all_gather | solution.py:191
  52.4 84.9 %all-gather.31.cloned.1.call-start = ((), (), s32[]{:S(2)}) async-start(), calls=%async_computation.9 | async-start | bytes 2654208 | tf_op jit(solution)/shard_map/all_gather | solution.py:191
  52.5 37.4 %collective-permute-start.2 = (bf16[256,1024]{1,0:T(8,128)(2,1)S(1)}, bf16[256,1024]{1,0:T(8,128)(2,1)S(1)}, u32[]{:S(2)}, u32[]{:S(2)}) collective-permute-start(bf16[256,1024]{1,0:T(8,128)(2,1)S(1)} %bitcast.68), channel_id=1, source_target_pairs={{8,0},{9,1},{10,2},{11,3},{12,4},{13,5},{14,6},{15,7}} | collective-permute-start | bytes 1572872 | tf_op jit(solution)/shard_map/ppermute | solution.py:177
  87.3 2.7 collective-permute-start.9
  93.6 74.6 %all-gather.17.cloned.1.call-start = ((), (), s32[]{:S(2)}) async-start(), calls=%async_computation.2 | async-start | bytes 2654208 | tf_op jit(solution)/shard_map/all_gather | solution.py:191
  122.4 76.6 %all-gather.33.cloned.1.call-start = ((), (), s32[]{:S(2)}) async-start(), calls=%async_computation.10 | async-start | bytes 2654208 | tf_op jit(solution)/shard_map/all_gather | solution.py:191
  122.5 28.0 %collective-permute-start.1 = (bf16[256,1024]{1,0:T(8,128)(2,1)S(1)}, bf16[256,1024]{1,0:T(8,128)(2,1)S(1)}, u32[]{:S(2)}, u32[]{:S(2)}) collective-permute-start(bf16[256,1024]{1,0:T(8,128)(2,1)S(1)} %bitcast.69), channel_id=1, source_target_pairs={{16,0},{17,1},{18,2},{19,3},{20,4},{21,5},{22,6},{23,7}} | collective-permute-start | bytes 1572872 | tf_op jit(solution)/shard_map/ppermute | solution.py:177
  149.2 10.6 %collective-permute-start.10 = (bf16[128,1024]{1,0:T(8,128)(2,1)}, bf16[128,1024]{1,0:T(8,128)(2,1)S(1)}, u32[]{:S(2)}, u32[]{:S(2)}) collective-permute-start(bf16[128,1024]{1,0:T(8,128)(2,1)} %layer.22), channel_id=1, source_target_pairs={{0,8},{8,16},{1,9},{9,17},{2,10},{10,18},{3,11},{11,19},{4,12},{12... | collective-permute-start | bytes 786440 | tf_op jit(solution)/shard_map/ppermute | solution.py:219
  163.2 66.5 %all-gather.19.cloned.1.call-start = ((), (), s32[]{:S(2)}) async-start(), calls=%async_computation.3 | async-start | bytes 2654208 | tf_op jit(solution)/shard_map/all_gather | solution.py:191
  180.0 10.6 %collective-permute-start.4 = (bf16[128,1024]{1,0:T(8,128)(2,1)}, bf16[128,1024]{1,0:T(8,128)(2,1)S(1)}, u32[]{:S(2)}, u32[]{:S(2)}) collective-permute-start(bf16[128,1024]{1,0:T(8,128)(2,1)} %layer.15), channel_id=1, source_target_pairs={{0,8},{8,16},{1,9},{9,17},{2,10},{10,18},{3,11},{11,19},{4,12},{12... | collective-permute-start | bytes 786440 | tf_op jit(solution)/shard_map/ppermute | solution.py:219
  194.0 66.7 %all-gather.35.cloned.1.call-start = ((), (), s32[]{:S(2)}) async-start(), calls=%async_computation.11 | async-start | bytes 2654208 | tf_op jit(solution)/shard_map/all_gather | solution.py:191
  194.1 20.1 %collective-permute-start = (bf16[256,1024]{1,0:T(8,128)(2,1)S(1)}, bf16[256,1024]{1,0:T(8,128)(2,1)S(1)}, u32[]{:S(2)}, u32[]{:S(2)}) collective-permute-start(bf16[256,1024]{1,0:T(8,128)(2,1)S(1)} %bitcast.70), channel_id=1, source_target_pairs={{24,0},{25,1},{26,2},{27,3},{28,4},{29,5},{30,6},{31,7}} | collective-permute-start | bytes 1572872 | tf_op jit(solution)/shard_map/ppermute | solution.py:177
  210.8 10.6 %collective-permute-start.11 = (bf16[128,1024]{1,0:T(8,128)(2,1)}, bf16[128,1024]{1,0:T(8,128)(2,1)S(1)}, u32[]{:S(2)}, u32[]{:S(2)}) collective-permute-start(bf16[128,1024]{1,0:T(8,128)(2,1)} %layer.23), channel_id=1, source_target_pairs={{0,8},{8,16},{16,24},{1,9},{9,17},{17,25},{2,10},{10,18},{18,26},{... | collective-permute-start | bytes 786440 | tf_op jit(solution)/shard_map/ppermute | solution.py:219
  224.8 66.8 %all-gather.21.cloned.1.call-start = ((), (), s32[]{:S(2)}) async-start(), calls=%async_computation.4 | async-start | bytes 2654208 | tf_op jit(solution)/shard_map/all_gather | solution.py:191
  241.6 10.6 %collective-permute-start.5 = (bf16[128,1024]{1,0:T(8,128)(2,1)}, bf16[128,1024]{1,0:T(8,128)(2,1)S(1)}, u32[]{:S(2)}, u32[]{:S(2)}) collective-permute-start(bf16[128,1024]{1,0:T(8,128)(2,1)} %layer.16), channel_id=1, source_target_pairs={{0,8},{8,16},{16,24},{1,9},{9,17},{17,25},{2,10},{10,18},{18,26},{... | collective-permute-start | bytes 786440 | tf_op jit(solution)/shard_map/ppermute | solution.py:219
  255.6 67.5 %all-gather.37.cloned.1.call-start = ((), (), s32[]{:S(2)}) async-start(), calls=%async_computation.12 | async-start | bytes 2654208 | tf_op jit(solution)/shard_map/all_gather | solution.py:191
  272.5 10.6 %collective-permute-start.12 = (bf16[128,1024]{1,0:T(8,128)(2,1)}, bf16[128,1024]{1,0:T(8,128)(2,1)S(1)}, u32[]{:S(2)}, u32[]{:S(2)}) collective-permute-start(bf16[128,1024]{1,0:T(8,128)(2,1)} %layer.24), channel_id=1, source_target_pairs={{0,8},{8,16},{16,24},{1,9},{9,17},{17,25},{2,10},{10,18},{18,26},{... | collective-permute-start | bytes 786440 | tf_op jit(solution)/shard_map/ppermute | solution.py:219
  286.5 67.5 %all-gather.23.cloned.1.call-start = ((), (), s32[]{:S(2)}) async-start(), calls=%async_computation.5 | async-start | bytes 2654208 | tf_op jit(solution)/shard_map/all_gather | solution.py:191
  303.4 10.6 %collective-permute-start.6 = (bf16[128,1024]{1,0:T(8,128)(2,1)}, bf16[128,1024]{1,0:T(8,128)(2,1)S(1)}, u32[]{:S(2)}, u32[]{:S(2)}) collective-permute-start(bf16[128,1024]{1,0:T(8,128)(2,1)} %layer.17), channel_id=1, source_target_pairs={{0,8},{8,16},{16,24},{1,9},{9,17},{17,25},{2,10},{10,18},{18,26},{... | collective-permute-start | bytes 786440 | tf_op jit(solution)/shard_map/ppermute | solution.py:219
  317.4 68.1 %all-gather.39.cloned.1.call-start = ((), (), s32[]{:S(2)}) async-start(), calls=%async_computation.13 | async-start | bytes 2654208 | tf_op jit(solution)/shard_map/all_gather | solution.py:191
  334.9 10.6 %collective-permute-start.13 = (bf16[128,1024]{1,0:T(8,128)(2,1)}, bf16[128,1024]{1,0:T(8,128)(2,1)S(1)}, u32[]{:S(2)}, u32[]{:S(2)}) collective-permute-start(bf16[128,1024]{1,0:T(8,128)(2,1)} %layer.25), channel_id=1, source_target_pairs={{8,16},{16,24},{9,17},{17,25},{10,18},{18,26},{11,19},{19,27},{12,... | collective-permute-start | bytes 786440 | tf_op jit(solution)/shard_map/ppermute | solution.py:219
  348.9 67.3 %all-gather.25.cloned.1.call-start = ((), (), s32[]{:S(2)}) async-start(), calls=%async_computation.6 | async-start | bytes 2654208 | tf_op jit(solution)/shard_map/all_gather | solution.py:191
  365.7 10.6 %collective-permute-start.7 = (bf16[128,1024]{1,0:T(8,128)(2,1)}, bf16[128,1024]{1,0:T(8,128)(2,1)S(1)}, u32[]{:S(2)}, u32[]{:S(2)}) collective-permute-start(bf16[128,1024]{1,0:T(8,128)(2,1)} %layer.18), channel_id=1, source_target_pairs={{8,16},{16,24},{9,17},{17,25},{10,18},{18,26},{11,19},{19,27},{12,... | collective-permute-start | bytes 786440 | tf_op jit(solution)/shard_map/ppermute | solution.py:219
  379.7 67.5 %all-gather.41.cloned.1.call-start = ((), (), s32[]{:S(2)}) async-start(), calls=%async_computation.14 | async-start | bytes 2654208 | tf_op jit(solution)/shard_map/all_gather | solution.py:191
  397.2 9.7 %collective-permute-start.14 = (bf16[128,1024]{1,0:T(8,128)(2,1)}, bf16[128,1024]{1,0:T(8,128)(2,1)S(1)}, u32[]{:S(2)}, u32[]{:S(2)}) collective-permute-start(bf16[128,1024]{1,0:T(8,128)(2,1)} %layer.26), channel_id=1, source_target_pairs={{16,24},{17,25},{18,26},{19,27},{20,28},{21,29},{22,30},{23,31}} | collective-permute-start | bytes 786440 | tf_op jit(solution)/shard_map/ppermute | solution.py:219
  410.3 67.6 %all-gather.27.cloned.1.call-start = ((), (), s32[]{:S(2)}) async-start(), calls=%async_computation.7 | async-start | bytes 2654208 | tf_op jit(solution)/shard_map/all_gather | solution.py:191
  428.1 9.8 %collective-permute-start.8 = (bf16[128,1024]{1,0:T(8,128)(2,1)}, bf16[128,1024]{1,0:T(8,128)(2,1)S(1)}, u32[]{:S(2)}, u32[]{:S(2)}) collective-permute-start(bf16[128,1024]{1,0:T(8,128)(2,1)} %layer.19), channel_id=1, source_target_pairs={{16,24},{17,25},{18,26},{19,27},{20,28},{21,29},{22,30},{23,31}} | collective-permute-start | bytes 786440 | tf_op jit(solution)/shard_map/ppermute | solution.py:219
  441.5 48.3 %collective-permute-start.17 = (bf16[256,1024]{1,0:T(8,128)(2,1)S(1)}, bf16[256,1024]{1,0:T(8,128)(2,1)S(1)}, u32[]{:S(2)}, u32[]{:S(2)}) collective-permute-start(bf16[256,1024]{1,0:T(8,128)(2,1)S(1)} %pad_maximum_fusion.2), channel_id=1, source_target_pairs={{24,0},{25,1},{26,2},{27,3},{28,4},{29,5},{30,6},{31,7}} | collective-permute-start | bytes 1572872 | tf_op jit(solution)/shard_map/ppermute | solution.py:230
  442.3 47.5 %collective-permute-start.16 = (bf16[256,1024]{1,0:T(8,128)(2,1)S(1)}, bf16[256,1024]{1,0:T(8,128)(2,1)S(1)}, u32[]{:S(2)}, u32[]{:S(2)}) collective-permute-start(bf16[256,1024]{1,0:T(8,128)(2,1)S(1)} %pad_maximum_fusion.1), channel_id=1, source_target_pairs={{24,8},{25,9},{26,10},{27,11},{28,12},{29,13},{30,14},{31,15}} | collective-permute-start | bytes 1572872 | tf_op jit(solution)/shard_map/ppermute | solution.py:230
  443.8 46.0 %collective-permute-start.15 = (bf16[256,1024]{1,0:T(8,128)(2,1)}, bf16[256,1024]{1,0:T(8,128)(2,1)S(1)}, u32[]{:S(2)}, u32[]{:S(2)}) collective-permute-start(bf16[256,1024]{1,0:T(8,128)(2,1)} %pad_maximum_fusion), channel_id=1, source_target_pairs={{24,16},{25,17},{26,18},{27,19},{28,20},{29,21},{30,22},{31,23}} | collective-permute-start | bytes 1572872 | tf_op jit(solution)/shard_map/ppermute | solution.py:230
  (29 other events, 139.3 us)
Sparse Core Ops, SparseCore 0:
  47.2 28.2 all-gather.28
  77.4 29.0 all-gather.14
  108.3 29.0 all-gather.30
  139.1 29.0 all-gather.16
  169.9 29.0 all-gather.32
  200.7 29.0 all-gather.18
  231.6 29.0 all-gather.34
  262.6 29.0 all-gather.20
  294.1 29.0 all-gather.36
  324.9 29.0 all-gather.22
  356.4 29.0 all-gather.38
  387.2 29.0 all-gather.24
  418.1 29.0 all-gather.40
  448.9 29.0 all-gather.26

commit v2 on v1

v2 whole, which is shorter than its diff:
```python
import functools

import jax
import jax.numpy as jnp
from jax import lax
from jax.experimental import pallas as pl
from jax.experimental.pallas import tpu as pltpu
from jax.sharding import PartitionSpec as P

BLOCK = 128
SIDE = 128
LAG = 2


def prep_kernel(rank, block, s_ref, *refs):
    *sources, gain_ref, table_ref, x_ref, m_ref = refs
    copies = m_ref.shape[0]
    rows, piece = x_ref.shape
    picked = [source[b * rows : (b + 1) * rows, :] for source, b in zip(sources, block)]
    if len(picked) == 2:
        x = jnp.where(s_ref[1] == 0, picked[0].astype(jnp.float32), picked[1].astype(jnp.float32))
    else:
        x = picked[0].astype(jnp.float32)
    x_ref[...] = x.astype(jnp.bfloat16)
    scaled = (x * gain_ref[...].astype(jnp.float32)).astype(jnp.bfloat16)
    squares = jnp.sum(x * x, axis=1, keepdims=True)
    high = squares.astype(jnp.bfloat16).astype(jnp.float32)
    low = squares - high
    inner = lax.dot_general(
        scaled, table_ref[s_ref[0]], (((1,), (1,)), ((), ())), preferred_element_type=jnp.float32
    )
    lane = lax.broadcasted_iota(jnp.int32, inner.shape, 1)
    side = jnp.where(lane < rank, inner, jnp.where(lane == rank, high, jnp.where(lane == rank + 1, low, 0.0)))
    side = side[:, :SIDE].astype(jnp.bfloat16)
    for copy in range(copies):
        m_ref[copy, :, :piece] = scaled
        m_ref[copy, :, piece:] = side


VMEM = pl.BlockSpec(memory_space=pltpu.VMEM)
SMEM = pl.BlockSpec(memory_space=pltpu.SMEM)


def near(x):
    return pltpu.with_memory_space_constraint(x, pltpu.VMEM)


def prep(scalars, sources, block, gain, table, rank, copies):
    piece = gain.shape[1]
    rows = BLOCK
    return pl.pallas_call(
        functools.partial(prep_kernel, rank, block),
        out_shape=(
            pltpu.VMEM((rows, piece), jnp.bfloat16),
            pltpu.VMEM((copies, rows, piece + SIDE), jnp.bfloat16),
        ),
        in_specs=[SMEM] + [VMEM] * (len(sources) + 2),
        out_specs=(VMEM, VMEM),
        compiler_params=pltpu.CompilerParams(vmem_limit_bytes=8 << 20),
        cost_estimate=pl.CostEstimate(
            flops=2 * rows * piece * SIDE, bytes_accessed=rows * piece * 8, transcendentals=0
        ),
        name="prep",
    )(scalars, *map(near, sources), near(gain), near(table))


def stage_kernel(w_ref, o_ref, sem):
    copy = pltpu.make_async_copy(w_ref, o_ref, sem)
    copy.start()
    copy.wait()


def staged(weight):
    return pl.pallas_call(
        stage_kernel,
        out_shape=pltpu.VMEM(weight.shape, weight.dtype),
        in_specs=[pl.BlockSpec(memory_space=pl.ANY)],
        out_specs=VMEM,
        scratch_shapes=[pltpu.SemaphoreType.DMA],
        compiler_params=pltpu.CompilerParams(vmem_limit_bytes=4 << 20),
        cost_estimate=pl.CostEstimate(flops=0, bytes_accessed=2 * weight.size, transcendentals=0),
        name="stage",
    )(weight)


def layer_kernel(rank, counts, s_ref, *refs):
    *parts, w_ref, x_ref, table_ref, o_ref = refs
    rows, piece = x_ref.shape
    width = w_ref.shape[0]
    side = jnp.zeros((rows, SIDE), jnp.float32)
    for part, count in zip(parts, counts):
        for k in range(count):
            side = side + part[k, :, piece:].astype(jnp.float32)
    squares = side[:, rank : rank + 1] + side[:, rank + 1 : rank + 2]
    scale = lax.rsqrt(squares / width + 1e-05)
    inner = (2.0 * side[:, :rank]).astype(jnp.bfloat16)
    tile = min(piece, 256)

    @pl.loop(0, piece // tile)
    def _(n):
        columns = pl.ds(pl.multiple_of(n * tile, tile), tile)
        total = jnp.dot(
            inner, table_ref[s_ref[0], rank : 2 * rank, columns], preferred_element_type=jnp.float32
        )
        i = 0
        for part, count in zip(parts, counts):
            for k in range(count):
                depth = pl.ds(pl.multiple_of(s_ref[2 + i] * piece, piece), piece)
                total += jnp.dot(
                    part[k, :, :piece], w_ref[depth, columns], preferred_element_type=jnp.float32
                )
                i += 1
        h = x_ref[:, columns].astype(jnp.float32)
        o_ref[:, columns] = (h + scale * total).astype(jnp.bfloat16)


def layer(scalars, parts, weight, x, table, rank):
    rows, piece = x.shape
    width = weight.shape[0]
    counts = tuple(part.shape[0] for part in parts)
    return pl.pallas_call(
        functools.partial(layer_kernel, rank, counts),
        out_shape=pltpu.VMEM((rows, piece), jnp.bfloat16),
        in_specs=[SMEM] + [VMEM] * (len(parts) + 3),
        out_specs=VMEM,
        compiler_params=pltpu.CompilerParams(vmem_limit_bytes=8 << 20),
        cost_estimate=pl.CostEstimate(
            flops=2 * rows * width * piece, bytes_accessed=2 * width * piece // 4, transcendentals=0
        ),
        name="layer",
    )(scalars, *map(near, parts), near(weight), near(x), near(table))


def shards(
    entering_hidden,
    section_weight,
    section_norm_gain,
    plugin_narrowing_factors,
    plugin_widening_factors,
    reward_head,
    adapter_of_block,
    live_block_rows,
):
    sections = lax.axis_size("section")
    section = lax.axis_index("section")
    chips = lax.axis_size("chip")
    cores = lax.axis_size("core")
    owners = chips * cores
    everyone = ("chip", "core")
    batches_here, rows, piece = entering_hidden.shape
    micro = batches_here * sections
    per_micro = rows // BLOCK
    owned = plugin_narrowing_factors.shape[1]
    rank = plugin_narrowing_factors.shape[3]
    weight = staged(section_weight[0])
    chunks = micro * per_micro

    down = jnp.swapaxes(plugin_narrowing_factors[0], 1, 2)
    maps = jnp.concatenate([down, plugin_widening_factors[0]], axis=1)
    maps = jnp.moveaxis(maps.reshape(owned, 2 * rank, owners, piece), 2, 0)
    table = lax.all_to_all(maps, everyone, split_axis=0, concat_axis=0, tiled=True)
    table = table.reshape(owners * owned, 2 * rank, piece)

    feeds = []
    for m in range(micro):
        home, slot = divmod(m, batches_here)
        block = entering_hidden[slot]
        feeds.append(block if home == 0 else lax.ppermute(block, "section", [(home, 0)]))

    adapters = adapter_of_block.reshape(-1)
    chip, core = lax.axis_index("chip"), lax.axis_index("core")
    base = jnp.arange(chips, dtype=jnp.int32) * cores
    order = jnp.concatenate([base + (core + k) % cores for k in range(cores)])

    def gathered(message):
        parts = lax.all_to_all(message, "chip", split_axis=0, concat_axis=0, tiled=True)
        out = [parts]
        for k in range(1, cores):
            out.append(lax.ppermute(parts, "core", [((c + k) % cores, c) for c in range(cores)]))
        return out

    arrived = {}
    done = {}
    zero = jnp.zeros((BLOCK, piece), jnp.bfloat16)
    for tick in range(chunks + LAG * (sections - 1)):
        active = [s for s in range(sections) if 0 <= tick - LAG * s < chunks]
        mine = jnp.clip(tick - LAG * section, 0, chunks - 1)
        adapter = lax.dynamic_index_in_dim(adapters, mine, 0, keepdims=True)
        scalars = jnp.concatenate([adapter, section[None].astype(jnp.int32), order])
        sources, blocks = [], []
        if 0 in active:
            m, b = divmod(tick, per_micro)
            sources.append(feeds[m])
            blocks.append(b)
        if active != [0]:
            sources.append(arrived.pop(tick, zero))
            blocks.append(0)
        x, message = prep(scalars, sources, blocks, section_norm_gain, table, rank, chips)
        parts = gathered(message)
        h = layer(scalars, parts, weight, x, table, rank)
        onward = [(s, s + 1) for s in active if s + 1 < sections]
        if onward:
            arrived[tick + LAG] = lax.ppermute(h, "section", onward)
        if sections - 1 in active:
            done[tick - LAG * (sections - 1)] = h

    slots = []
    for slot in range(batches_here):
        value = None
        for home in range(sections):
            m = home * batches_here + slot
            block = jnp.concatenate([done[m * per_micro + b] for b in range(per_micro)], axis=0)
            if home != sections - 1:
                block = lax.ppermute(block, "section", [(sections - 1, home)])
            value = block if value is None else jnp.where(section == home, block, value)
        slots.append(value)
    hidden_out = jnp.stack(slots)
    partial_score = jnp.sum(
        hidden_out.astype(jnp.float32) * reward_head.astype(jnp.float32)[None, None, :], axis=2
    )
    raw = lax.psum(partial_score, everyone)
    place = jnp.arange(rows, dtype=jnp.int32) % BLOCK
    limits = jnp.repeat(live_block_rows, BLOCK, axis=1)
    scores = jnp.where(place[None, :] < limits, raw, jnp.float32(0.0))
    return (hidden_out, scores)


def solution(mesh):
    sections, owners = mesh.shape["section"], mesh.shape["mp"]
    cores = 2 if owners % 2 == 0 else 1
    fine = jax.sharding.Mesh(
        mesh.devices.reshape(sections, owners // cores, cores), ("section", "chip", "core")
    )
    mp = ("chip", "core")
    placed = (
        P("section", None, mp),
        P("section", None, mp),
        P("section", mp),
        P("section", mp, None, None),
        P("section", mp, None, None),
        P(mp),
        P(),
        P("section", None),
    )
    return jax.shard_map(
        shards,
        mesh=fine,
        in_specs=placed,
        out_specs=(P("section", None, mp), P("section", None)),
        check_vma=False,
    )
```

time: 516 us -> 566 us (1.097)
  Pallas kernels: 203 us -> 79 us
  local copies, waits for them, and re-layouts: 15.9 us -> 113 us
  blocking collectives: 13.1 us -> 75.6 us
  starting transfers between devices: 51.2 us -> 103 us
  waiting for transfers between devices: 198 us -> 173 us
  between operations: 14.4 us -> 1.89 us
    pallas_call x28 -> x29, Pallas kernels: 203 us -> 79 us  [the longest x14 66 us: layer(): pl.pallas_call(functools.partial(layer_kernel, rank, counts), out_shape=p...]
    all_gather x14 -> x0, waiting for transfers between devices: 106 us -> none  [gathered(): return [lax.all_gather(message, everyone, axis=0, tiled=True)]]
    unnamed x59 -> x195, local copies, waits for them, and re-layouts: 12.6 us -> 110 us
    all_to_all x0 -> x11, waiting for transfers between devices: none -> 67.5 us  [gathered(): lax.all_to_all(message, 'chip', split_axis=0, concat_axis=0, tiled=True)]
    all_to_all x0 -> x3, blocking collectives: none -> 62.9 us  [gathered(): lax.all_to_all(message, 'chip', split_axis=0, concat_axis=0, tiled=True)]
    all_to_all x0 -> x11, starting transfers between devices: none -> 42.2 us  [gathered(): lax.all_to_all(message, 'chip', split_axis=0, concat_axis=0, tiled=True)]
    ppermute x3, waiting for transfers between devices: 0.01 us -> 17.5 us  [shards(): block = lax.ppermute(block, 'section', [(sections - 1, home)])]
    concatenate x5 -> x7, other arithmetic: 12.2 us -> 10.3 us  [shards(): scalars = jnp.concatenate([adapter, section[None].astype(jnp.int32), order])]
  transfers between devices with their start and end apart: 33 -> 44, of which waited for: 25 -> 18; matrix products, arithmetic and copies ran while one was open for 3% -> 3% of each run, Pallas kernels for 39% -> 14%
where the time goes in v2:
time: 566 us; the launch traced here: 563 us
  waiting for transfers between devices  173 us (31%)
  local copies, waits for them, and re-layouts  113 us (20%)
  starting transfers between devices  103 us (18%)
  Pallas kernels  79 us (14%)
  blocking collectives  75.6 us (13%)
  other arithmetic  17 us (3%)
    unnamed x195, local copies, waits for them, and re-layouts  110 us
    all_to_all x11, waiting for transfers between devices, gathered(): lax.all_to_all(message, 'chip', split_axis=0, concat_axis=0, tiled=True)  67.5 us
    pallas_call x14, Pallas kernels, layer(): pl.pallas_call(functools.partial(layer_kernel, rank, counts), out_shape=p...  66 us
    ppermute x12, waiting for transfers between devices, shards(): arrived[tick + LAG] = lax.ppermute(h, 'section', onward)  64.4 us
    all_to_all x3, blocking collectives, gathered(): lax.all_to_all(message, 'chip', split_axis=0, concat_axis=0, tiled=True)  62.9 us
    all_to_all x11, starting transfers between devices, gathered(): lax.all_to_all(message, 'chip', split_axis=0, concat_axis=0, tiled=True)  42.2 us
    ppermute x12, starting transfers between devices, shards(): arrived[tick + LAG] = lax.ppermute(h, 'section', onward)  33.5 us
    all_to_all x1, waiting for transfers between devices, shards(): lax.all_to_all(maps, everyone, split_axis=0, concat_axis=0, tiled=True)  23.9 us
  transfers between devices with their start and end apart: 44, of which 18 were waited for; matrix products, arithmetic and copies ran while one was open for 3% of the time, Pallas kernels for 14%

profile of v2, /device:TPU:16, one launch (start us, length us, event | category | flops | bytes accessed | tf_op | source)
XLA Modules:
  0.0 562.8 jit_solution(862589619278284026)
XLA Ops:
  12.5 23.9 %all-to-all-done = bf16[8,1,128,1024]{3,2,1,0:T(8,128)(2,1)S(1)} async-done(((bf16[8,1,128,1024]{3,2,1,0:T(8,128)(2,1)}), bf16[8,1,128,1024]{3,2,1,0:T(8,128)(2,1)S(1)}, u32[]{:S(2)}, u32[]{:S(2)}) %all-to-all-start) | async-done | bytes 2097184 | tf_op jit(solution)/shard_map/all_to_all | solution.py:161
  46.7 10.1 %all-to-all-done.8.refs_0_ = bf16[4,128,1152]{2,1,0:T(8,128)(2,1)S(1)} async-done(((bf16[4,128,1152]{2,1,0:T(8,128)(2,1)}), bf16[4,128,1152]{2,1,0:T(8,128)(2,1)S(1)}, u32[]{:S(2)}, u32[]{:S(2)}) %all-to-all-start.8) | async-done | bytes 1179680 | tf_op jit(solution)/shard_map/all_to_all | solution.py:176
  56.8 21.0 %all_to_all.75.refs_0_ = bf16[4,128,1152]{2,1,0:T(8,128)(2,1)} all-to-all(bf16[4,128,1152]{2,1,0:T(8,128)(2,1)} %copy-done.37), channel_id=1, replica_groups=mesh['section'=4,'chip'=4,'core'=2] {'chip'}, dimensions={0} | all-to-all | bytes 2359296 | tf_op jit(solution)/shard_map/all_to_all | solution.py:176
  78.5 5.8 %copy-done.13 = bf16[1,8192,1024]{2,1,0:T(8,128)(2,1)S(1)} copy-done((bf16[1,8192,1024]{2,1,0:T(8,128)(2,1)S(1)}, bf16[1,8192,1024]{2,1,0:T(8,128)(2,1)}, u32[]{:S(2)}) %copy-start.13) | copy-done | bytes 16777240
  100.0 5.8 %copy-done.1 = bf16[8192,1024]{1,0:T(8,128)(2,1)S(1)} copy-done((bf16[8192,1024]{1,0:T(8,128)(2,1)S(1)}, bf16[8192,1024]{1,0:T(8,128)(2,1)}, u32[]{:S(2)}) %copy-start.1) | copy-done | bytes 16777240
  115.9 21.0 %all_to_all.76.refs_0_ = bf16[4,128,1152]{2,1,0:T(8,128)(2,1)} all-to-all(bf16[4,128,1152]{2,1,0:T(8,128)(2,1)} %copy-done.35), channel_id=1, replica_groups=mesh['section'=4,'chip'=4,'core'=2] {'chip'}, dimensions={0} | all-to-all | bytes 2359296 | tf_op jit(solution)/shard_map/all_to_all | solution.py:176
  136.9 17.0 %collective-permute-start.1 = (bf16[256,1024]{1,0:T(8,128)(2,1)S(1)}, bf16[256,1024]{1,0:T(8,128)(2,1)S(1)}, u32[]{:S(2)}, u32[]{:S(2)}) collective-permute-start(bf16[256,1024]{1,0:T(8,128)(2,1)S(1)} %bitcast.55), channel_id=1, source_target_pairs={{16,0},{17,1},{18,2},{19,3},{20,4},{21,5},{22,6},{23,7}} | collective-permute-start | bytes 1572872 | tf_op jit(solution)/shard_map/ppermute | solution.py:168
  154.0 5.8 %copy-done.2 = bf16[8192,1024]{1,0:T(8,128)(2,1)S(1)} copy-done((bf16[8192,1024]{1,0:T(8,128)(2,1)S(1)}, bf16[8192,1024]{1,0:T(8,128)(2,1)}, u32[]{:S(2)}) %copy-start.2) | copy-done | bytes 16777240
  166.3 7.7 %collective-permute-done.19.refs_1_ = bf16[128,1024]{1,0:T(8,128)(2,1)S(1)} collective-permute-done((bf16[128,1024]{1,0:T(8,128)(2,1)S(1)}, bf16[128,1024]{1,0:T(8,128)(2,1)S(1)}, u32[]{:S(2)}, u32[]{:S(2)}) %collective-permute-start.19) | collective-permute-done | bytes 262176 | tf_op jit(solution)/shard_map/ppermute | solution.py:203
  180.2 5.8 %copy-done.3 = bf16[8192,1024]{1,0:T(8,128)(2,1)S(1)} copy-done((bf16[8192,1024]{1,0:T(8,128)(2,1)S(1)}, bf16[8192,1024]{1,0:T(8,128)(2,1)}, u32[]{:S(2)}) %copy-start.3) | copy-done | bytes 16777240
  193.0 8.2 %collective-permute-done.6.refs_1_ = bf16[128,1024]{1,0:T(8,128)(2,1)S(1)} collective-permute-done((bf16[128,1024]{1,0:T(8,128)(2,1)S(1)}, bf16[128,1024]{1,0:T(8,128)(2,1)S(1)}, u32[]{:S(2)}, u32[]{:S(2)}) %collective-permute-start.6) | collective-permute-done | bytes 262176 | tf_op jit(solution)/shard_map/ppermute | solution.py:203
  207.4 13.9 %all-to-all-done.3.refs_0_ = bf16[4,128,1152]{2,1,0:T(8,128)(2,1)} async-done(((bf16[4,128,1152]{2,1,0:T(8,128)(2,1)}), bf16[4,128,1152]{2,1,0:T(8,128)(2,1)}, u32[]{:S(2)}, u32[]{:S(2)}) %all-to-all-start.3) | async-done | bytes 1179680 | tf_op jit(solution)/shard_map/all_to_all | solution.py:176
  222.1 5.8 %copy-done.4 = bf16[8192,1024]{1,0:T(8,128)(2,1)S(1)} copy-done((bf16[8192,1024]{1,0:T(8,128)(2,1)S(1)}, bf16[8192,1024]{1,0:T(8,128)(2,1)}, u32[]{:S(2)}) %copy-start.4) | copy-done | bytes 16777240
  238.4 6.3 %collective-permute-done.21.refs_1_ = bf16[128,1024]{1,0:T(8,128)(2,1)S(1)} collective-permute-done((bf16[128,1024]{1,0:T(8,128)(2,1)S(1)}, bf16[128,1024]{1,0:T(8,128)(2,1)S(1)}, u32[]{:S(2)}, u32[]{:S(2)}) %collective-permute-start.21) | collective-permute-done | bytes 262176 | tf_op jit(solution)/shard_map/ppermute | solution.py:203
  251.0 5.8 %copy-done.5 = bf16[8192,1024]{1,0:T(8,128)(2,1)S(1)} copy-done((bf16[8192,1024]{1,0:T(8,128)(2,1)S(1)}, bf16[8192,1024]{1,0:T(8,128)(2,1)}, u32[]{:S(2)}) %copy-start.5) | copy-done | bytes 16777240
  265.9 5.8 %collective-permute-done.8.refs_1_ = bf16[128,1024]{1,0:T(8,128)(2,1)S(1)} collective-permute-done((bf16[128,1024]{1,0:T(8,128)(2,1)S(1)}, bf16[128,1024]{1,0:T(8,128)(2,1)S(1)}, u32[]{:S(2)}, u32[]{:S(2)}) %collective-permute-start.8) | collective-permute-done | bytes 262176 | tf_op jit(solution)/shard_map/ppermute | solution.py:203
  278.6 14.3 %all-to-all-done.4.refs_0_ = bf16[4,128,1152]{2,1,0:T(8,128)(2,1)} async-done(((bf16[4,128,1152]{2,1,0:T(8,128)(2,1)}), bf16[4,128,1152]{2,1,0:T(8,128)(2,1)}, u32[]{:S(2)}, u32[]{:S(2)}) %all-to-all-start.4) | async-done | bytes 1179680 | tf_op jit(solution)/shard_map/all_to_all | solution.py:176
  292.9 5.8 %copy-done.6 = bf16[8192,1024]{1,0:T(8,128)(2,1)S(1)} copy-done((bf16[8192,1024]{1,0:T(8,128)(2,1)S(1)}, bf16[8192,1024]{1,0:T(8,128)(2,1)}, u32[]{:S(2)}) %copy-start.6) | copy-done | bytes 16777240
  307.7 7.3 %collective-permute-done.23.refs_0_ = bf16[128,1024]{1,0:T(8,128)(2,1)S(1)} collective-permute-done((bf16[128,1024]{1,0:T(8,128)(2,1)S(1)}, bf16[128,1024]{1,0:T(8,128)(2,1)S(1)}, u32[]{:S(2)}, u32[]{:S(2)}) %collective-permute-start.23) | collective-permute-done | bytes 262176 | tf_op jit(solution)/shard_map/ppermute | solution.py:203
  321.1 5.8 %copy-done.7 = bf16[8192,1024]{1,0:T(8,128)(2,1)S(1)} copy-done((bf16[8192,1024]{1,0:T(8,128)(2,1)S(1)}, bf16[8192,1024]{1,0:T(8,128)(2,1)}, u32[]{:S(2)}) %copy-start.7) | copy-done | bytes 16777240
  349.6 14.3 %all-to-all-done.5.refs_0_ = bf16[4,128,1152]{2,1,0:T(8,128)(2,1)} async-done(((bf16[4,128,1152]{2,1,0:T(8,128)(2,1)}), bf16[4,128,1152]{2,1,0:T(8,128)(2,1)}, u32[]{:S(2)}, u32[]{:S(2)}) %all-to-all-start.5) | async-done | bytes 1179680 | tf_op jit(solution)/shard_map/all_to_all | solution.py:176
  364.0 5.8 %copy-done.8 = bf16[8192,1024]{1,0:T(8,128)(2,1)S(1)} copy-done((bf16[8192,1024]{1,0:T(8,128)(2,1)S(1)}, bf16[8192,1024]{1,0:T(8,128)(2,1)}, u32[]{:S(2)}) %copy-start.8) | copy-done | bytes 16777240
  378.7 7.3 %collective-permute-done.25.refs_0_ = bf16[128,1024]{1,0:T(8,128)(2,1)S(1)} collective-permute-done((bf16[128,1024]{1,0:T(8,128)(2,1)S(1)}, bf16[128,1024]{1,0:T(8,128)(2,1)S(1)}, u32[]{:S(2)}, u32[]{:S(2)}) %collective-permute-start.25) | collective-permute-done | bytes 262176 | tf_op jit(solution)/shard_map/ppermute | solution.py:203
  392.3 5.8 %copy-done.9 = bf16[8192,1024]{1,0:T(8,128)(2,1)S(1)} copy-done((bf16[8192,1024]{1,0:T(8,128)(2,1)S(1)}, bf16[8192,1024]{1,0:T(8,128)(2,1)}, u32[]{:S(2)}) %copy-start.9) | copy-done | bytes 16777240
  416.5 21.0 %all_to_all.77.refs_0_ = bf16[4,128,1152]{2,1,0:T(8,128)(2,1)} all-to-all(bf16[4,128,1152]{2,1,0:T(8,128)(2,1)} %copy-done.36), channel_id=1, replica_groups=mesh['section'=4,'chip'=4,'core'=2] {'chip'}, dimensions={0} | all-to-all | bytes 2359296 | tf_op jit(solution)/shard_map/all_to_all | solution.py:176
  437.5 5.8 %copy-done.10 = bf16[8192,1024]{1,0:T(8,128)(2,1)S(1)} copy-done((bf16[8192,1024]{1,0:T(8,128)(2,1)S(1)}, bf16[8192,1024]{1,0:T(8,128)(2,1)}, u32[]{:S(2)}) %copy-start.10) | copy-done | bytes 16777240
  450.6 6.2 %collective-permute-done.27.refs_0_ = bf16[128,1024]{1,0:T(8,128)(2,1)S(1)} collective-permute-done((bf16[128,1024]{1,0:T(8,128)(2,1)S(1)}, bf16[128,1024]{1,0:T(8,128)(2,1)S(1)}, u32[]{:S(2)}, u32[]{:S(2)}) %collective-permute-start.27) | collective-permute-done | bytes 262176 | tf_op jit(solution)/shard_map/ppermute | solution.py:203
  463.1 5.8 %copy-done.11 = bf16[8192,1024]{1,0:T(8,128)(2,1)S(1)} copy-done((bf16[8192,1024]{1,0:T(8,128)(2,1)S(1)}, bf16[8192,1024]{1,0:T(8,128)(2,1)}, u32[]{:S(2)}) %copy-start.11) | copy-done | bytes 16777240
  491.7 14.3 %all-to-all-done.7.refs_0_ = bf16[4,128,1152]{2,1,0:T(8,128)(2,1)} async-done(((bf16[4,128,1152]{2,1,0:T(8,128)(2,1)}), bf16[4,128,1152]{2,1,0:T(8,128)(2,1)}, u32[]{:S(2)}, u32[]{:S(2)}) %all-to-all-start.7) | async-done | bytes 1179680 | tf_op jit(solution)/shard_map/all_to_all | solution.py:176
  514.1 5.8 %copy-done.12 = bf16[8192,1024]{1,0:T(8,128)(2,1)S(1)} copy-done((bf16[8192,1024]{1,0:T(8,128)(2,1)S(1)}, bf16[8192,1024]{1,0:T(8,128)(2,1)}, u32[]{:S(2)}) %copy-start.12) | copy-done | bytes 16777240
  529.7 17.5 %collective-permute-done.29 = bf16[256,1024]{1,0:T(8,128)(2,1)} collective-permute-done((bf16[256,1024]{1,0:T(8,128)(2,1)}, bf16[256,1024]{1,0:T(8,128)(2,1)}, u32[]{:S(2)}, u32[]{:S(2)}) %collective-permute-start.29) | collective-permute-done | bytes 524320 | tf_op jit(solution)/shard_map/ppermute | solution.py:214
  549.5 12.7 %psum.7 = f32[1,256]{1,0:T(1,128)S(1)} all-reduce(f32[1,256]{1,0:T(1,128)S(1)} %bitcast.61), channel_id=1, replica_groups=mesh['section'=4,'chip'=4,'core'=2] {'chip','core'}, use_global_device_ids=true, to_apply=%region_1.2 | all-reduce | flops 256 | bytes 2048 | tf_op jit(solution)/shard_map/psum | solution.py:221
  (303 shorter events, 236.5 us)
Async XLA Ops:
  5.8 30.5 %all-to-all-start = ((bf16[8,1,128,1024]{3,2,1,0:T(8,128)(2,1)}), bf16[8,1,128,1024]{3,2,1,0:T(8,128)(2,1)S(1)}, u32[]{:S(2)}, u32[]{:S(2)}) async-start(bf16[8,1,128,1024]{3,2,1,0:T(8,128)(2,1)} %copy.15), calls=%async_computation | async-start | bytes 4194304 | tf_op jit(solution)/shard_map/all_to_all | solution.py:161
  38.9 17.8 %all-to-all-start.8 = ((bf16[4,128,1152]{2,1,0:T(8,128)(2,1)}), bf16[4,128,1152]{2,1,0:T(8,128)(2,1)S(1)}, u32[]{:S(2)}, u32[]{:S(2)}) async-start(bf16[4,128,1152]{2,1,0:T(8,128)(2,1)} %copy-done.34), calls=%async_computation.8 | async-start | bytes 2359296 | tf_op jit(solution)/shard_map/all_to_all | solution.py:176
  56.8 28.6 %collective-permute-start.16 = (bf16[4,128,1152]{2,1,0:T(8,128)(2,1)S(1)}, bf16[4,128,1152]{2,1,0:T(8,128)(2,1)S(1)}, u32[]{:S(2)}, u32[]{:S(2)}) collective-permute-start(bf16[4,128,1152]{2,1,0:T(8,128)(2,1)S(1)} %all-to-all-done.8.refs_0_), channel_id=1, source_target_pairs={{1,0},{0,1},{3,2},{2,3},{5,4},{4,5},{7,6},{6,7},{9,8},{8,9},{11,10... | collective-permute-start | bytes 3538952 | tf_op jit(solution)/shard_map/ppermute | solution.py:179
  77.8 22.2 %collective-permute-start.3 = (bf16[4,128,1152]{2,1,0:T(8,128)(2,1)}, bf16[4,128,1152]{2,1,0:T(8,128)(2,1)}, u32[]{:S(2)}, u32[]{:S(2)}) collective-permute-start(bf16[4,128,1152]{2,1,0:T(8,128)(2,1)} %all_to_all.75.refs_0_), channel_id=1, source_target_pairs={{1,0},{0,1},{3,2},{2,3},{5,4},{4,5},{7,6},{6,7},{9,8},{8,9},{11,10... | collective-permute-start | bytes 3538952 | tf_op jit(solution)/shard_map/ppermute | solution.py:179
  77.8 16.1 %collective-permute-start.2 = (bf16[256,1024]{1,0:T(8,128)(2,1)S(1)}, bf16[256,1024]{1,0:T(8,128)(2,1)S(1)}, u32[]{:S(2)}, u32[]{:S(2)}) collective-permute-start(bf16[256,1024]{1,0:T(8,128)(2,1)S(1)} %bitcast.54), channel_id=1, source_target_pairs={{8,0},{9,1},{10,2},{11,3},{12,4},{13,5},{14,6},{15,7}} | collective-permute-start | bytes 1572872 | tf_op jit(solution)/shard_map/ppermute | solution.py:168
  96.4 19.5 %all-to-all-start.9 = ((bf16[4,128,1152]{2,1,0:T(8,128)(2,1)}), bf16[4,128,1152]{2,1,0:T(8,128)(2,1)S(1)}, u32[]{:S(2)}, u32[]{:S(2)}) async-start(bf16[4,128,1152]{2,1,0:T(8,128)(2,1)} %copy-done.25), calls=%async_computation.9 | async-start | bytes 2359296 | tf_op jit(solution)/shard_map/all_to_all | solution.py:176
  115.9 38.0 %collective-permute-start.18 = (bf16[4,128,1152]{2,1,0:T(8,128)(2,1)S(1)}, bf16[4,128,1152]{2,1,0:T(8,128)(2,1)S(1)}, u32[]{:S(2)}, u32[]{:S(2)}) collective-permute-start(bf16[4,128,1152]{2,1,0:T(8,128)(2,1)S(1)} %all-to-all-done.9.refs_0_), channel_id=1, source_target_pairs={{1,0},{0,1},{3,2},{2,3},{5,4},{4,5},{7,6},{6,7},{9,8},{8,9},{11,10... | collective-permute-start | bytes 3538952 | tf_op jit(solution)/shard_map/ppermute | solution.py:179
  136.9 43.3 %collective-permute-start.5 = (bf16[4,128,1152]{2,1,0:T(8,128)(2,1)}, bf16[4,128,1152]{2,1,0:T(8,128)(2,1)}, u32[]{:S(2)}, u32[]{:S(2)}) collective-permute-start(bf16[4,128,1152]{2,1,0:T(8,128)(2,1)} %all_to_all.76.refs_0_), channel_id=1, source_target_pairs={{1,0},{0,1},{3,2},{2,3},{5,4},{4,5},{7,6},{6,7},{9,8},{8,9},{11,10... | collective-permute-start | bytes 3538952 | tf_op jit(solution)/shard_map/ppermute | solution.py:179
  136.9 29.4 %collective-permute-start.1 = (bf16[256,1024]{1,0:T(8,128)(2,1)S(1)}, bf16[256,1024]{1,0:T(8,128)(2,1)S(1)}, u32[]{:S(2)}, u32[]{:S(2)}) collective-permute-start(bf16[256,1024]{1,0:T(8,128)(2,1)S(1)} %bitcast.55), channel_id=1, source_target_pairs={{16,0},{17,1},{18,2},{19,3},{20,4},{21,5},{22,6},{23,7}} | collective-permute-start | bytes 1572872 | tf_op jit(solution)/shard_map/ppermute | solution.py:168
  176.6 26.4 %all-to-all-start.10 = ((bf16[4,128,1152]{2,1,0:T(8,128)(2,1)}), bf16[4,128,1152]{2,1,0:T(8,128)(2,1)S(1)}, u32[]{:S(2)}, u32[]{:S(2)}) async-start(bf16[4,128,1152]{2,1,0:T(8,128)(2,1)} %copy-done.27), calls=%async_computation.10 | async-start | bytes 2359296 | tf_op jit(solution)/shard_map/all_to_all | solution.py:176
  203.0 18.3 %all-to-all-start.3 = ((bf16[4,128,1152]{2,1,0:T(8,128)(2,1)}), bf16[4,128,1152]{2,1,0:T(8,128)(2,1)}, u32[]{:S(2)}, u32[]{:S(2)}) async-start(bf16[4,128,1152]{2,1,0:T(8,128)(2,1)} %copy-done.30), calls=%async_computation.3 | async-start | bytes 2359296 | tf_op jit(solution)/shard_map/all_to_all | solution.py:176
  207.3 14.7 %collective-permute-start.20 = (bf16[4,128,1152]{2,1,0:T(8,128)(2,1)S(1)}, bf16[4,128,1152]{2,1,0:T(8,128)(2,1)}, u32[]{:S(2)}, u32[]{:S(2)}) collective-permute-start(bf16[4,128,1152]{2,1,0:T(8,128)(2,1)S(1)} %all-to-all-done.10.refs_0_), channel_id=1, source_target_pairs={{1,0},{0,1},{3,2},{2,3},{5,4},{4,5},{7,6},{6,7},{9,8},{8,9},{11,10... | collective-permute-start | bytes 3538952 | tf_op jit(solution)/shard_map/ppermute | solution.py:179
  221.4 29.6 %collective-permute-start.7 = (bf16[4,128,1152]{2,1,0:T(8,128)(2,1)}, bf16[4,128,1152]{2,1,0:T(8,128)(2,1)}, u32[]{:S(2)}, u32[]{:S(2)}) collective-permute-start(bf16[4,128,1152]{2,1,0:T(8,128)(2,1)} %all-to-all-done.3.refs_0_), channel_id=1, source_target_pairs={{1,0},{0,1},{3,2},{2,3},{5,4},{4,5},{7,6},{6,7},{9,8},{8,9},{11,10... | collective-permute-start | bytes 3538952 | tf_op jit(solution)/shard_map/ppermute | solution.py:179
  221.4 17.0 %collective-permute-start = (bf16[256,1024]{1,0:T(8,128)(2,1)}, bf16[256,1024]{1,0:T(8,128)(2,1)S(1)}, u32[]{:S(2)}, u32[]{:S(2)}) collective-permute-start(bf16[256,1024]{1,0:T(8,128)(2,1)} %bitcast.51), channel_id=1, source_target_pairs={{24,0},{25,1},{26,2},{27,3},{28,4},{29,5},{30,6},{31,7}} | collective-permute-start | bytes 1572872 | tf_op jit(solution)/shard_map/ppermute | solution.py:168
  247.2 26.3 %all-to-all-start.11 = ((bf16[4,128,1152]{2,1,0:T(8,128)(2,1)}), bf16[4,128,1152]{2,1,0:T(8,128)(2,1)S(1)}, u32[]{:S(2)}, u32[]{:S(2)}) async-start(bf16[4,128,1152]{2,1,0:T(8,128)(2,1)} %copy-done.28), calls=%async_computation.11 | async-start | bytes 2359296 | tf_op jit(solution)/shard_map/all_to_all | solution.py:176
  274.2 18.7 %all-to-all-start.4 = ((bf16[4,128,1152]{2,1,0:T(8,128)(2,1)}), bf16[4,128,1152]{2,1,0:T(8,128)(2,1)}, u32[]{:S(2)}, u32[]{:S(2)}) async-start(bf16[4,128,1152]{2,1,0:T(8,128)(2,1)} %copy-done.31), calls=%async_computation.4 | async-start | bytes 2359296 | tf_op jit(solution)/shard_map/all_to_all | solution.py:176
  278.5 14.4 %collective-permute-start.22 = (bf16[4,128,1152]{2,1,0:T(8,128)(2,1)S(1)}, bf16[4,128,1152]{2,1,0:T(8,128)(2,1)}, u32[]{:S(2)}, u32[]{:S(2)}) collective-permute-start(bf16[4,128,1152]{2,1,0:T(8,128)(2,1)S(1)} %all-to-all-done.11.refs_0_), channel_id=1, source_target_pairs={{1,0},{0,1},{3,2},{2,3},{5,4},{4,5},{7,6},{6,7},{9,8},{8,9},{11,10... | collective-permute-start | bytes 3538952 | tf_op jit(solution)/shard_map/ppermute | solution.py:179
  292.9 28.2 %collective-permute-start.9 = (bf16[4,128,1152]{2,1,0:T(8,128)(2,1)}, bf16[4,128,1152]{2,1,0:T(8,128)(2,1)}, u32[]{:S(2)}, u32[]{:S(2)}) collective-permute-start(bf16[4,128,1152]{2,1,0:T(8,128)(2,1)} %all-to-all-done.4.refs_0_), channel_id=1, source_target_pairs={{1,0},{0,1},{3,2},{2,3},{5,4},{4,5},{7,6},{6,7},{9,8},{8,9},{11,10... | collective-permute-start | bytes 3538952 | tf_op jit(solution)/shard_map/ppermute | solution.py:179
  317.5 27.8 %all-to-all-start.12 = ((bf16[4,128,1152]{2,1,0:T(8,128)(2,1)}), bf16[4,128,1152]{2,1,0:T(8,128)(2,1)S(1)}, u32[]{:S(2)}, u32[]{:S(2)}) async-start(bf16[4,128,1152]{2,1,0:T(8,128)(2,1)} %copy-done.26), calls=%async_computation.12 | async-start | bytes 2359296 | tf_op jit(solution)/shard_map/all_to_all | solution.py:176
  345.3 18.7 %all-to-all-start.5 = ((bf16[4,128,1152]{2,1,0:T(8,128)(2,1)}), bf16[4,128,1152]{2,1,0:T(8,128)(2,1)}, u32[]{:S(2)}, u32[]{:S(2)}) async-start(bf16[4,128,1152]{2,1,0:T(8,128)(2,1)} %copy-done.32), calls=%async_computation.5 | async-start | bytes 2359296 | tf_op jit(solution)/shard_map/all_to_all | solution.py:176
  349.6 14.4 %collective-permute-start.24 = (bf16[4,128,1152]{2,1,0:T(8,128)(2,1)S(1)}, bf16[4,128,1152]{2,1,0:T(8,128)(2,1)}, u32[]{:S(2)}, u32[]{:S(2)}) collective-permute-start(bf16[4,128,1152]{2,1,0:T(8,128)(2,1)S(1)} %all-to-all-done.12.refs_0_), channel_id=1, source_target_pairs={{1,0},{0,1},{3,2},{2,3},{5,4},{4,5},{7,6},{6,7},{9,8},{8,9},{11,10... | collective-permute-start | bytes 3538952 | tf_op jit(solution)/shard_map/ppermute | solution.py:179
  364.0 28.3 %collective-permute-start.11 = (bf16[4,128,1152]{2,1,0:T(8,128)(2,1)}, bf16[4,128,1152]{2,1,0:T(8,128)(2,1)}, u32[]{:S(2)}, u32[]{:S(2)}) collective-permute-start(bf16[4,128,1152]{2,1,0:T(8,128)(2,1)} %all-to-all-done.5.refs_0_), channel_id=1, source_target_pairs={{1,0},{0,1},{3,2},{2,3},{5,4},{4,5},{7,6},{6,7},{9,8},{8,9},{11,10... | collective-permute-start | bytes 3538952 | tf_op jit(solution)/shard_map/ppermute | solution.py:179
  388.6 27.9 %all-to-all-start.13 = ((bf16[4,128,1152]{2,1,0:T(8,128)(2,1)}), bf16[4,128,1152]{2,1,0:T(8,128)(2,1)S(1)}, u32[]{:S(2)}, u32[]{:S(2)}) async-start(bf16[4,128,1152]{2,1,0:T(8,128)(2,1)} %copy-done.24), calls=%async_computation.13 | async-start | bytes 2359296 | tf_op jit(solution)/shard_map/all_to_all | solution.py:176
  416.5 21.0 %collective-permute-start.26 = (bf16[4,128,1152]{2,1,0:T(8,128)(2,1)S(1)}, bf16[4,128,1152]{2,1,0:T(8,128)(2,1)S(1)}, u32[]{:S(2)}, u32[]{:S(2)}) collective-permute-start(bf16[4,128,1152]{2,1,0:T(8,128)(2,1)S(1)} %all-to-all-done.13.refs_0_), channel_id=1, source_target_pairs={{1,0},{0,1},{3,2},{2,3},{5,4},{4,5},{7,6},{6,7},{9,8},{8,9},{11,10... | collective-permute-start | bytes 3538952 | tf_op jit(solution)/shard_map/ppermute | solution.py:179
  437.5 25.6 %collective-permute-start.13 = (bf16[4,128,1152]{2,1,0:T(8,128)(2,1)}, bf16[4,128,1152]{2,1,0:T(8,128)(2,1)}, u32[]{:S(2)}, u32[]{:S(2)}) collective-permute-start(bf16[4,128,1152]{2,1,0:T(8,128)(2,1)} %all_to_all.77.refs_0_), channel_id=1, source_target_pairs={{1,0},{0,1},{3,2},{2,3},{5,4},{4,5},{7,6},{6,7},{9,8},{8,9},{11,10... | collective-permute-start | bytes 3538952 | tf_op jit(solution)/shard_map/ppermute | solution.py:179
  459.4 27.9 %all-to-all-start.14 = ((bf16[4,128,1152]{2,1,0:T(8,128)(2,1)}), bf16[4,128,1152]{2,1,0:T(8,128)(2,1)S(1)}, u32[]{:S(2)}, u32[]{:S(2)}) async-start(bf16[4,128,1152]{2,1,0:T(8,128)(2,1)} %copy-done.29), calls=%async_computation.14 | async-start | bytes 2359296 | tf_op jit(solution)/shard_map/all_to_all | solution.py:176
  487.4 18.7 %all-to-all-start.7 = ((bf16[4,128,1152]{2,1,0:T(8,128)(2,1)}), bf16[4,128,1152]{2,1,0:T(8,128)(2,1)}, u32[]{:S(2)}, u32[]{:S(2)}) async-start(bf16[4,128,1152]{2,1,0:T(8,128)(2,1)} %copy-done.33), calls=%async_computation.7 | async-start | bytes 2359296 | tf_op jit(solution)/shard_map/all_to_all | solution.py:176
  491.7 22.4 %collective-permute-start.28 = (bf16[4,128,1152]{2,1,0:T(8,128)(2,1)S(1)}, bf16[4,128,1152]{2,1,0:T(8,128)(2,1)}, u32[]{:S(2)}, u32[]{:S(2)}) collective-permute-start(bf16[4,128,1152]{2,1,0:T(8,128)(2,1)S(1)} %all-to-all-done.14.refs_0_), channel_id=1, source_target_pairs={{1,0},{0,1},{3,2},{2,3},{5,4},{4,5},{7,6},{6,7},{9,8},{8,9},{11,10... | collective-permute-start | bytes 3538952 | tf_op jit(solution)/shard_map/ppermute | solution.py:179
  506.1 18.6 %collective-permute-start.15 = (bf16[4,128,1152]{2,1,0:T(8,128)(2,1)}, bf16[4,128,1152]{2,1,0:T(8,128)(2,1)}, u32[]{:S(2)}, u32[]{:S(2)}) collective-permute-start(bf16[4,128,1152]{2,1,0:T(8,128)(2,1)} %all-to-all-done.7.refs_0_), channel_id=1, source_target_pairs={{1,0},{0,1},{3,2},{2,3},{5,4},{4,5},{7,6},{6,7},{9,8},{8,9},{11,10... | collective-permute-start | bytes 3538952 | tf_op jit(solution)/shard_map/ppermute | solution.py:179
  508.0 21.7 %collective-permute-start.31 = (bf16[256,1024]{1,0:T(8,128)(2,1)}, bf16[256,1024]{1,0:T(8,128)(2,1)}, u32[]{:S(2)}, u32[]{:S(2)}) collective-permute-start(bf16[256,1024]{1,0:T(8,128)(2,1)} %pad_maximum_fusion.2), channel_id=1, source_target_pairs={{24,0},{25,1},{26,2},{27,3},{28,4},{29,5},{30,6},{31,7}} | collective-permute-start | bytes 1572872 | tf_op jit(solution)/shard_map/ppermute | solution.py:214
  510.5 19.2 %collective-permute-start.30 = (bf16[256,1024]{1,0:T(8,128)(2,1)}, bf16[256,1024]{1,0:T(8,128)(2,1)}, u32[]{:S(2)}, u32[]{:S(2)}) collective-permute-start(bf16[256,1024]{1,0:T(8,128)(2,1)} %pad_maximum_fusion.1), channel_id=1, source_target_pairs={{24,8},{25,9},{26,10},{27,11},{28,12},{29,13},{30,14},{31,15}} | collective-permute-start | bytes 1572872 | tf_op jit(solution)/shard_map/ppermute | solution.py:214
  512.8 34.4 %collective-permute-start.29 = (bf16[256,1024]{1,0:T(8,128)(2,1)}, bf16[256,1024]{1,0:T(8,128)(2,1)}, u32[]{:S(2)}, u32[]{:S(2)}) collective-permute-start(bf16[256,1024]{1,0:T(8,128)(2,1)} %pad_maximum_fusion), channel_id=1, source_target_pairs={{24,16},{25,17},{26,18},{27,19},{28,20},{29,21},{30,22},{31,23}} | collective-permute-start | bytes 1572872 | tf_op jit(solution)/shard_map/ppermute | solution.py:214
  (108 other events, 749.6 us)
